TPU v7x, 32 devices: a whole 2x2x4 slice. The times are simulated.
32 devices in a mesh: dp: 8 (over z, x), tensor: 4 (over y, core).
Axes of the slice: x: 2, y: 2, z: 4, core: 2. Of those that a mesh axis runs over, the one named last changes fastest.
Arguments:
- inputs: bfloat16 [4096, 768], P(('dp', 'tensor')), may hold values from -6 to 6
- seq_lengths: int32 [8, 2], P('dp'), may hold values from 0 to 512, as said below
- attn_gain: bfloat16 [768], P('dp'), may hold values from 0.25 to 1.75
- wqkv: bfloat16 [768, 3, 768], P('dp', None, 'tensor'), may hold values from -0.21875 to 0.21875
- wo: bfloat16 [768, 768], P('tensor', 'dp'), may hold values from -2.5 to 2.5
- mlp_gain: bfloat16 [768], P('dp'), may hold values from 0.25 to 1.75
- wi: bfloat16 [768, 2, 1152], P('dp', None, 'tensor'), may hold values from -0.21875 to 0.21875
- wo2: bfloat16 [1152, 768], P('tensor', 'dp'), may hold values from -0.1875 to 0.1875
- cotangent: bfloat16 [4096, 768], P(('dp', 'tensor')), may hold values from -6 to 6
Outputs:
- output: bfloat16 [4096, 768], P(('dp', 'tensor'))
- input_grad: bfloat16 [4096, 768], P(('dp', 'tensor'))
- attn_gain_grad: float32 [768], P('dp')
- wqkv_grad: float32 [768, 3, 768], P('dp', None, 'tensor')
- wo_grad: float32 [768, 768], P('tensor', 'dp')
- mlp_gain_grad: float32 [768], P('dp')
- wi_grad: float32 [768, 2, 1152], P('dp', None, 'tensor')
- wo2_grad: float32 [1152, 768], P('tensor', 'dp')
Inputs may be any that keep to these rules, and one draw needn't show every extreme that they name: Row g of seq_lengths lists the sequences packed from the first row of group g on; the lengths of a row sum to at most 512. In one row a single sequence fills all 512 rows and the other length is 0.
All inputs are finite; a program needn't handle non-finite values.
Results may differ from a plain program's by a relative error of at most 0.02.
Values may be sent and summed in bfloat16 or wider, within the bound.
A program may use at most 64 MiB of HBM per device.

v0:
```python
import jax
import jax.numpy as jnp
from jax import lax
from jax.sharding import PartitionSpec as P

HEAD_DIM = 64
SEQS = 2


NORM_EPS = 1e-05
ROPE_THETA = 160000.0
SCORE_SCALE = 0.125


def layout(lengths, row_count):
    seq_ends = jnp.cumsum(lengths)
    row_ids = jnp.arange(row_count, dtype=jnp.int32)
    segment = jnp.sum((row_ids[None, :] >= seq_ends[:, None]).astype(jnp.int32), axis=0)
    starts = jnp.concatenate([seq_ends - lengths, seq_ends[-1:]])
    slot_ids = jnp.arange(lengths.shape[0] + 1, dtype=jnp.int32)
    seq_begin = jnp.sum(
        jnp.where(segment[None, :] == slot_ids[:, None], starts[:, None], 0), axis=0
    )
    return (segment, row_ids - seq_begin)


def normalize(array_in, gain_vec):
    row_mean = jnp.mean(array_in, axis=-1, keepdims=True)
    centred = array_in - row_mean
    spread = jnp.mean(centred * centred, axis=-1, keepdims=True)
    return centred * lax.rsqrt(spread + NORM_EPS) * gain_vec


def rotation(position):
    half_dim = HEAD_DIM // 2
    frequency = ROPE_THETA ** (-jnp.arange(half_dim, dtype=jnp.float32) / half_dim)
    angles = position.astype(jnp.float32)[:, None] * frequency[None, :]
    return (jnp.cos(angles)[:, None, :], jnp.sin(angles)[:, None, :])


def rotate(array_in, cosine, sine_table):
    half_dim = HEAD_DIM // 2
    first_half = array_in[..., :half_dim]
    second_half = array_in[..., half_dim:]
    return jnp.concatenate(
        [
            first_half * cosine - second_half * sine_table,
            second_half * cosine + first_half * sine_table,
        ],
        axis=-1,
    )


def rotate_back(array_in, cosine, sine_table):
    half_dim = HEAD_DIM // 2
    first_half = array_in[..., :half_dim]
    second_half = array_in[..., half_dim:]
    return jnp.concatenate(
        [
            first_half * cosine + second_half * sine_table,
            second_half * cosine - first_half * sine_table,
        ],
        axis=-1,
    )


def gated_gelu(first_half, second_half):
    return jax.nn.gelu(first_half, approximate=False) * second_half


def gather_rows(array_in):
    return lax.all_gather(array_in, "tensor", axis=0, tiled=True)


def sum_rows(array_in):
    return lax.psum_scatter(
        array_in.astype(jnp.bfloat16), "tensor", scatter_dimension=0, tiled=True
    ).astype(jnp.float32)


def masked_scores(query_part, key_low, segment_part, segment):
    scores = (
        jnp.einsum("qhd,khd->hqk", query_part, key_low, preferred_element_type=jnp.float32)
        * SCORE_SCALE
    )
    same_seq = segment_part[:, None] == segment[None, :]
    return jnp.where(same_seq[None], scores, -1e30)


def shards(inputs, seq_lengths, attn_gain, wqkv, wo, mlp_gain, wi, wo2, cotangent):
    local_rows = inputs.shape[0]
    tensor_rank = lax.axis_index("tensor")
    group_rows = local_rows * lax.axis_size("tensor")
    segment, position = layout(seq_lengths[0], group_rows)
    own_segment = lax.dynamic_slice_in_dim(segment, tensor_rank * local_rows, local_rows)
    valid_rows = (own_segment < SEQS).astype(jnp.float32)[:, None]
    cosine, sine_table = rotation(position)
    full_qkv, full_wo, full_wi, full_wo2, gain_one, gain_two = (
        lax.all_gather(wqkv, "dp", axis=0, tiled=True),
        lax.all_gather(wo, "dp", axis=1, tiled=True),
        lax.all_gather(wi, "dp", axis=0, tiled=True),
        lax.all_gather(wo2, "dp", axis=1, tiled=True),
        lax.all_gather(attn_gain, "dp", axis=0, tiled=True),
        lax.all_gather(mlp_gain, "dp", axis=0, tiled=True),
    )
    model_width = full_qkv.shape[0]
    head_cols = full_qkv.shape[2]
    heads_here = head_cols // HEAD_DIM
    hidden_cols = full_wi.shape[2]
    x_value = inputs.astype(jnp.float32)
    attn_in = normalize(x_value, gain_one.astype(jnp.float32)).astype(jnp.bfloat16)
    attn_all = gather_rows(attn_in)
    qkv = jnp.dot(
        attn_all, full_qkv.reshape(model_width, 3 * head_cols), preferred_element_type=jnp.float32
    )
    qkv = qkv.reshape(group_rows, 3, heads_here, HEAD_DIM)
    query_low = rotate(qkv[:, 0], cosine, sine_table).astype(jnp.bfloat16)
    key_low = rotate(qkv[:, 1], cosine, sine_table).astype(jnp.bfloat16)
    value_low = qkv[:, 2].astype(jnp.bfloat16)
    block_rows = min(512, group_rows)
    block_count = group_rows // block_rows
    query_blocks = query_low.reshape(block_count, block_rows, heads_here, HEAD_DIM)
    segment_blocks = segment.reshape(block_count, block_rows)

    def forward_block(pieces):
        scores = masked_scores(pieces[0], key_low, pieces[1], segment)
        row_max = jnp.max(scores, axis=-1, keepdims=True)
        exponent = jnp.exp(scores - row_max)
        row_total = jnp.sum(exponent, axis=-1, keepdims=True)
        prob_low = (exponent / row_total).astype(jnp.bfloat16)
        context_part = jnp.einsum(
            "hqk,khd->qhd", prob_low, value_low, preferred_element_type=jnp.float32
        )
        return (context_part.astype(jnp.bfloat16), (row_max + jnp.log(row_total))[..., 0])

    context, log_total = lax.map(forward_block, (query_blocks, segment_blocks))
    context = context.reshape(group_rows, head_cols)
    attn_out = sum_rows(jnp.dot(context, full_wo, preferred_element_type=jnp.float32))
    residual = x_value + attn_out
    mlp_in = normalize(residual, gain_two.astype(jnp.float32)).astype(jnp.bfloat16)
    mlp_all = gather_rows(mlp_in)
    projected = jnp.dot(
        mlp_all, full_wi.reshape(model_width, 2 * hidden_cols), preferred_element_type=jnp.float32
    )
    projected = projected.reshape(group_rows, 2, hidden_cols)
    hidden = gated_gelu(projected[:, 0], projected[:, 1]).astype(jnp.bfloat16)
    mlp_out = sum_rows(jnp.dot(hidden, full_wo2, preferred_element_type=jnp.float32))
    output = (valid_rows * (residual + mlp_out)).astype(jnp.bfloat16)
    back_qkv, back_wo, back_wi, back_wo2, back_one, back_two = (
        lax.all_gather(wqkv, "dp", axis=0, tiled=True),
        lax.all_gather(wo, "dp", axis=1, tiled=True),
        lax.all_gather(wi, "dp", axis=0, tiled=True),
        lax.all_gather(wo2, "dp", axis=1, tiled=True),
        lax.all_gather(attn_gain, "dp", axis=0, tiled=True),
        lax.all_gather(mlp_gain, "dp", axis=0, tiled=True),
    )
    grad_out = valid_rows * cotangent.astype(jnp.float32)
    grad_mlp_all = gather_rows(grad_out.astype(jnp.bfloat16))
    wo2_grad = jnp.einsum("gf,gd->fd", hidden, grad_mlp_all, preferred_element_type=jnp.float32)
    grad_hidden = jnp.einsum(
        "gd,fd->gf", grad_mlp_all, back_wo2, preferred_element_type=jnp.float32
    )
    unused_value, gelu_pull = jax.vjp(gated_gelu, projected[:, 0], projected[:, 1])
    grad_first, grad_second = gelu_pull(grad_hidden)
    grad_proj = (
        jnp.stack([grad_first, grad_second], axis=1)
        .astype(jnp.bfloat16)
        .reshape(group_rows, 2 * hidden_cols)
    )
    wi_grad = jnp.einsum(
        "gd,gc->dc", mlp_all, grad_proj, preferred_element_type=jnp.float32
    ).reshape(model_width, 2, hidden_cols)
    grad_mlp_in = sum_rows(
        jnp.einsum(
            "gc,dc->gd",
            grad_proj,
            back_wi.reshape(model_width, 2 * hidden_cols),
            preferred_element_type=jnp.float32,
        )
    )
    unused_norm, second_pull = jax.vjp(normalize, residual, back_two.astype(jnp.float32))
    grad_residual_norm, mlp_gain_part = second_pull(grad_mlp_in)
    grad_residual = grad_out + grad_residual_norm
    grad_attn_all = gather_rows(grad_residual.astype(jnp.bfloat16))
    wo_grad = jnp.einsum("gc,gd->cd", context, grad_attn_all, preferred_element_type=jnp.float32)
    grad_context = jnp.einsum(
        "gd,cd->gc", grad_attn_all, back_wo, preferred_element_type=jnp.float32
    )
    grad_context = grad_context.astype(jnp.bfloat16).reshape(
        block_count, block_rows, heads_here, HEAD_DIM
    )

    def backward_block(carried, pieces):
        grad_key, grad_value = carried
        query_part, segment_part, grad_part, total_part = pieces
        scores = masked_scores(query_part, key_low, segment_part, segment)
        probs = jnp.exp(scores - total_part[..., None])
        prob_low = probs.astype(jnp.bfloat16)
        grad_value = grad_value + jnp.einsum(
            "hqk,qhd->khd", prob_low, grad_part, preferred_element_type=jnp.float32
        )
        grad_probs = jnp.einsum(
            "qhd,khd->hqk", grad_part, value_low, preferred_element_type=jnp.float32
        )
        row_inner = jnp.sum(probs * grad_probs, axis=-1, keepdims=True)
        grad_scores = (probs * (grad_probs - row_inner)).astype(jnp.bfloat16)
        grad_query = (
            jnp.einsum("hqk,khd->qhd", grad_scores, key_low, preferred_element_type=jnp.float32)
            * SCORE_SCALE
        )
        grad_key = (
            grad_key
            + jnp.einsum(
                "hqk,qhd->khd", grad_scores, query_part, preferred_element_type=jnp.float32
            )
            * SCORE_SCALE
        )
        return ((grad_key, grad_value), grad_query)

    zero_rows = jnp.zeros((group_rows, heads_here, HEAD_DIM), jnp.float32)
    (grad_key, grad_value), grad_query = lax.scan(
        backward_block,
        (zero_rows, zero_rows),
        (query_blocks, segment_blocks, grad_context, log_total),
    )
    grad_query = grad_query.reshape(group_rows, heads_here, HEAD_DIM)
    grad_qkv = jnp.stack(
        [
            rotate_back(grad_query, cosine, sine_table),
            rotate_back(grad_key, cosine, sine_table),
            grad_value,
        ],
        axis=1,
    )
    grad_qkv = grad_qkv.astype(jnp.bfloat16).reshape(group_rows, 3 * head_cols)
    wqkv_grad = jnp.einsum(
        "gd,gc->dc", attn_all, grad_qkv, preferred_element_type=jnp.float32
    ).reshape(model_width, 3, head_cols)
    grad_attn_in = sum_rows(
        jnp.einsum(
            "gc,dc->gd",
            grad_qkv,
            back_qkv.reshape(model_width, 3 * head_cols),
            preferred_element_type=jnp.float32,
        )
    )
    unused_first, first_pull = jax.vjp(normalize, x_value, back_one.astype(jnp.float32))
    grad_input_norm, attn_gain_part = first_pull(grad_attn_in)
    input_grad = (grad_residual + grad_input_norm).astype(jnp.bfloat16)
    gain_one_sum, gain_two_sum = lax.psum((attn_gain_part, mlp_gain_part), "tensor")
    wqkv_sent, wo_sent, wi_sent, wo2_sent, one_sent, two_sent = (
        lax.psum_scatter(wqkv_grad, "dp", scatter_dimension=0, tiled=True),
        lax.psum_scatter(wo_grad, "dp", scatter_dimension=1, tiled=True),
        lax.psum_scatter(wi_grad, "dp", scatter_dimension=0, tiled=True),
        lax.psum_scatter(wo2_grad, "dp", scatter_dimension=1, tiled=True),
        lax.psum_scatter(gain_one_sum, "dp", scatter_dimension=0, tiled=True),
        lax.psum_scatter(gain_two_sum, "dp", scatter_dimension=0, tiled=True),
    )
    return (output, input_grad, one_sent, wqkv_sent, wo_sent, two_sent, wi_sent, wo2_sent)


def solution(mesh):
    in_specs = (
        P(("dp", "tensor"), None),
        P("dp", None),
        P("dp"),
        P("dp", None, "tensor"),
        P("tensor", "dp"),
        P("dp"),
        P("dp", None, "tensor"),
        P("tensor", "dp"),
        P(("dp", "tensor"), None),
    )
    out_specs = (
        P(("dp", "tensor"), None),
        P(("dp", "tensor"), None),
        P("dp"),
        P("dp", None, "tensor"),
        P("tensor", "dp"),
        P("dp"),
        P("dp", None, "tensor"),
        P("tensor", "dp"),
    )
    return jax.shard_map(shards, mesh=mesh, in_specs=in_specs, out_specs=out_specs, check_vma=False)
```

profile of v0, /device:TPU:11, one launch (start us, length us, event | category | flops | bytes accessed | tf_op | source)
XLA Modules:
  0.0 582.1 jit_solution(6712184240352297298)
XLA Ops:
  17.0 12.2 %all-reduce.6 = (bf16[768]{0:T(1024)(128)(2,1)S(1)}, bf16[768]{0:T(1024)(128)(2,1)}) all-reduce(bf16[768]{0:T(1024)(128)(2,1)S(1)} %dynamic-update-slice, bf16[768]{0:T(1024)(128)(2,1)S(1)} %dynamic-update-slice.1), channel_id=1, replica_groups=mesh['dp'=8,'tensor'=4] {'dp'}, use_global_device_ids=true, to_apply=%add | all-reduce | flops 1536 | bytes 6144
  31.2 27.1 %all_gather.39 = bf16[192,768]{0,1:T(8,128)(2,1)} all-gather(bf16[192,96]{0,1:T(8,128)(2,1)S(1)} %copy.51), channel_id=1, replica_groups=mesh['dp'=8,'tensor'=4] {'dp'}, dimensions={1}, use_global_device_ids=true | all-gather | bytes 331776 | tf_op jit(solution)/shard_map/all_gather | solution.py:100
  59.4 18.3 %all_gather.37 = bf16[512,768]{1,0:T(8,128)(2,1)S(1)} all-gather(bf16[128,768]{1,0:T(8,128)(2,1)S(1)} %fusion.50), channel_id=1, replica_groups=mesh['dp'=8,'tensor'=4] {'tensor'}, dimensions={0}, use_global_device_ids=true | all-gather | bytes 983040 | tf_op jit(solution)/shard_map/all_gather | solution.py:72
  77.7 38.5 %all_gather.38 = bf16[768,3,192]{2,1,0:T(4,128)(2,1)S(1)} all-gather(bf16[96,3,192]{2,1,0:T(4,128)(2,1)S(1)} %copy.48), channel_id=1, replica_groups=mesh['dp'=8,'tensor'=4] {'dp'}, dimensions={0}, use_global_device_ids=true | all-gather | bytes 995328 | tf_op jit(solution)/shard_map/all_gather | solution.py:99
  124.7 28.0 %all_gather.42 = bf16[768,2,288]{2,0,1:T(8,128)(2,1)} all-gather(bf16[96,2,288]{2,0,1:T(8,128)(2,1)S(1)} %copy.52), channel_id=1, replica_groups=mesh['dp'=8,'tensor'=4] {'dp'}, dimensions={0}, use_global_device_ids=true | all-gather | bytes 995328 | tf_op jit(solution)/shard_map/all_gather | solution.py:101
  152.7 2.3 copy.53
  155.0 24.6 %all_gather.43 = bf16[288,768]{0,1:T(8,128)(2,1)S(1)} all-gather(bf16[288,96]{0,1:T(8,128)(2,1)} %copy.54), channel_id=1, replica_groups=mesh['dp'=8,'tensor'=4] {'dp'}, dimensions={1}, use_global_device_ids=true | all-gather | bytes 497664 | tf_op jit(solution)/shard_map/all_gather | solution.py:102
  179.7 22.8 %all_gather.44 = bf16[512,768]{1,0:T(8,128)(2,1)S(1)} all-gather(bf16[128,768]{1,0:T(8,128)(2,1)S(1)} %fusion.56), channel_id=1, replica_groups=mesh['dp'=8,'tensor'=4] {'tensor'}, dimensions={0}, use_global_device_ids=true | all-gather | bytes 983040 | tf_op jit(solution)/shard_map/all_gather | solution.py:72
  208.2 8.7 %all_gather.41 = bf16[512,768]{1,0:T(8,128)(2,1)S(1)} all-gather(bf16[128,768]{1,0:T(8,128)(2,1)S(1)} %multiply_convert_fusion.3), channel_id=1, replica_groups=mesh['dp'=8,'tensor'=4] {'tensor'}, dimensions={0}, use_global_device_ids=true | all-gather | bytes 983040 | tf_op jit(solution)/shard_map/all_gather | solution.py:72
  220.9 1.8 bitcast_convert_fusion
  225.1 2.6 convolution_convert_fusion.2
  228.7 2.9 convolution_bitcast_fusion
  231.7 17.6 %reduce-scatter.17.cloned.1.call-done = bf16[128,768]{1,0:T(8,128)(2,1)} async-done(((bf16[512,768]{1,0:T(8,128)(2,1)}), bf16[128,768]{1,0:T(8,128)(2,1)}) %reduce-scatter.17.cloned.1.call-update) | async-done | bytes 196624 | tf_op jit(solution)/shard_map/reduce_scatter | solution.py:76
  249.2 1.8 fusion.52
  252.3 22.8 %reduce-scatter.15.cloned.1.call-done = bf16[128,768]{1,0:T(8,128)(2,1)} async-done(((bf16[512,768]{1,0:T(8,128)(2,1)}), bf16[128,768]{1,0:T(8,128)(2,1)}) %reduce-scatter.15.cloned.1.call-update) | async-done | bytes 196624 | tf_op jit(solution)/shard_map/reduce_scatter | solution.py:76
  275.1 2.0 fusion.73
  278.9 8.7 %all_gather.45 = bf16[512,768]{1,0:T(8,128)(2,1)S(1)} all-gather(bf16[128,768]{1,0:T(8,128)(2,1)S(1)} %fusion.60), channel_id=1, replica_groups=mesh['dp'=8,'tensor'=4] {'tensor'}, dimensions={0}, use_global_device_ids=true | all-gather | bytes 983040 | tf_op jit(solution)/shard_map/all_gather | solution.py:72
  289.5 1.7 multiply_reduce_fusion
  294.7 2.0 fusion.10
  298.9 1.7 convolution_convert_fusion
  300.8 2.2 fusion.18
  303.1 2.2 fusion.16
  306.1 34.7 %reduce-scatter.27.cloned.1.call-done = f32[96,288]{1,0:T(8,128)} async-done(((f32[768,288]{1,0:T(8,128)}), f32[96,288]{1,0:T(8,128)}) %reduce-scatter.27.cloned.1.call-update) | async-done | bytes 110608
  340.8 1.7 copy.73
  342.5 63.3 %reduce-scatter.25.cloned.1.call-done = f32[96,192]{1,0:T(8,128)} async-done(((f32[768,192]{1,0:T(8,128)}), f32[96,192]{1,0:T(8,128)}) %reduce-scatter.25.cloned.1.call-update) | async-done | bytes 73744
  407.4 25.0 %reduce-scatter.19.cloned.1.call-done = bf16[128,768]{1,0:T(8,128)(2,1)} async-done(((bf16[512,768]{1,0:T(8,128)(2,1)}), bf16[128,768]{1,0:T(8,128)(2,1)}) %reduce-scatter.19.cloned.1.call-update) | async-done | bytes 196624 | tf_op jit(solution)/shard_map/reduce_scatter | solution.py:76
  434.7 12.1 %all-reduce.4 = (f32[768]{0:T(1024)S(1)}, f32[768]{0:T(1024)S(1)}) all-reduce(f32[768]{0:T(1024)S(1)} %get-tuple-element.99, f32[768]{0:T(1024)S(1)} %copy-done.42), channel_id=6, replica_groups=mesh['dp'=8,'tensor'=4] {'dp'}, use_global_device_ids=true, to_apply=%region_20.21.clone | all-reduce | flops 1536 | bytes 12288
  447.0 9.6 %all-reduce.5 = (f32[96]{0:T(128)}, f32[96]{0:T(128)}) all-reduce(f32[96]{0:T(128)S(1)} %dynamic-slice.5, f32[96]{0:T(128)S(1)} %dynamic-slice.7), channel_id=1, replica_groups=mesh['dp'=8,'tensor'=4] {'tensor'}, use_global_device_ids=true, to_apply=%region_19.20 | all-reduce | flops 192 | bytes 1536 | tf_op jit(solution)/shard_map/psum | solution.py:250
  456.6 1.9 add_convert_fusion
  458.5 44.4 %reduce-scatter.23.cloned.1.call-done = f32[96,2,288]{2,0,1:T(8,128)} async-done(((f32[768,2,288]{2,0,1:T(8,128)}), f32[96,2,288]{2,0,1:T(8,128)}) %reduce-scatter.23.cloned.1.call-update) | async-done | bytes 221200 | tf_op jit(solution)/shard_map/reduce_scatter | solution.py:254
  502.8 1.9 copy.60
  504.7 70.5 %reduce-scatter.21.cloned.1.call-done = f32[96,3,192]{2,0,1:T(8,128)} async-done(((f32[768,3,192]{2,0,1:T(8,128)}), f32[96,3,192]{2,0,1:T(8,128)}) %reduce-scatter.21.cloned.1.call-update) | async-done | bytes 221200 | tf_op jit(solution)/shard_map/reduce_scatter | solution.py:252
  (192 shorter events, 48.3 us)
Async XLA Ops:
  7.2 197.6 %reduce-scatter.13.cloned.1.call-start = ((), (), s32[]{:S(2)}) async-start(), calls=%async_computation.8 | async-start | bytes 983040 | tf_op jit(solution)/shard_map/reduce_scatter | solution.py:76
  10.4 106.8 %copy-start.43 = (f32[128]{0:T(128)}, f32[128]{0:T(128)S(1)}, u32[]{:S(2)}) copy-start(f32[128]{0:T(128)S(1)} %broadcast_multiply_fusion.1) | copy-start | bytes 1540
  11.5 4.7 copy-start.52
  11.5 105.6 %copy-start.49 = (f32[128]{0:T(128)}, f32[128]{0:T(128)S(1)}, u32[]{:S(2)}) copy-start(f32[128]{0:T(128)S(1)} %fusion.66) | copy-start | bytes 1540
  77.7 40.1 %copy-start.3 = (bf16[512,768]{1,0:T(8,128)(2,1)}, bf16[512,768]{1,0:T(8,128)(2,1)S(1)}, u32[]{:S(2)}) copy-start(bf16[512,768]{1,0:T(8,128)(2,1)S(1)} %all_gather.37) | copy-start | bytes 2359300
  120.4 32.3 %copy-start.29 = (bf16[3,64,512]{2,1,0:T(8,128)(2,1)}, bf16[3,64,512]{2,1,0:T(8,128)(2,1)S(1)}, u32[]{:S(2)}) copy-start(bf16[3,64,512]{2,1,0:T(8,128)(2,1)S(1)} %fusion.11) | copy-start | bytes 589828
  122.0 57.6 %copy-start.22 = (bf16[128,768]{1,0:T(8,128)(2,1)S(1)}, bf16[128,768]{1,0:T(8,128)(2,1)}, u32[]{:S(2)}) copy-start(bf16[128,768]{1,0:T(8,128)(2,1)} %param.17) | copy-start | bytes 589828
  122.1 127.2 %reduce-scatter.17.cloned.1.call-start = ((), (), s32[]{:S(2)}) async-start(), calls=%async_computation.10 | async-start | bytes 983040 | tf_op jit(solution)/shard_map/reduce_scatter | solution.py:76
  155.0 49.8 %copy-start = (bf16[128,768]{1,0:T(8,128)(2,1)S(1)}, bf16[128,768]{1,0:T(8,128)(2,1)}, u32[]{:S(2)}) copy-start(bf16[128,768]{1,0:T(8,128)(2,1)} %param.9) | copy-start | bytes 589828
  155.0 52.0 %copy-start.45 = (f32[128]{0:T(128)}, f32[128]{0:T(128)S(1)}, u32[]{:S(2)}) copy-start(f32[128]{0:T(128)S(1)} %compare_convert_fusion.1) | copy-start | bytes 1540
  179.6 22.9 %copy-start.8 = (bf16[288,768]{0,1:T(8,128)(2,1)}, bf16[288,768]{0,1:T(8,128)(2,1)S(1)}, u32[]{:S(2)}) copy-start(bf16[288,768]{0,1:T(8,128)(2,1)S(1)} %all_gather.43) | copy-start | bytes 1327108
  204.7 13.0 %copy-start.16 = (bf16[768,2,288]{0,2,1:T(8,128)(2,1)S(1)}, bf16[768,2,288]{0,2,1:T(8,128)(2,1)}, u32[]{:S(2)}) copy-start(bf16[768,2,288]{0,2,1:T(8,128)(2,1)} %copy.53) | copy-start | bytes 2654212
  205.9 12.6 %copy-start.47 = (f32[128]{0:T(128)}, f32[128]{0:T(128)S(1)}, u32[]{:S(2)}) copy-start(f32[128]{0:T(128)S(1)} %broadcast_multiply_fusion) | copy-start | bytes 1540
  205.9 12.6 %copy-start.9 = (f32[512,288]{0,1:T(8,128)S(1)}, f32[512,288]{0,1:T(8,128)}, u32[]{:S(2)}) copy-start(f32[512,288]{0,1:T(8,128)} %fusion.77) | copy-start | bytes 1769476
  207.1 12.8 %copy-start.54 = (f32[128]{0:T(128)}, f32[128]{0:T(128)S(1)}, u32[]{:S(2)}) copy-start(f32[128]{0:T(128)S(1)} %multiply_reduce_fusion.1) | copy-start | bytes 1540
  207.1 12.8 %copy-start.48 = (f32[128]{0:T(128)}, f32[128]{0:T(128)S(1)}, u32[]{:S(2)}) copy-start(f32[128]{0:T(128)S(1)} %fusion.67) | copy-start | bytes 1540
  222.7 52.4 %reduce-scatter.15.cloned.1.call-start = ((), (), s32[]{:S(2)}) async-start(), calls=%async_computation.9 | async-start | bytes 983040 | tf_op jit(solution)/shard_map/reduce_scatter | solution.py:76
  227.7 21.6 %copy-start.11 = (bf16[128,768]{1,0:T(8,128)(2,1)S(1)}, bf16[128,768]{1,0:T(8,128)(2,1)}, u32[]{:S(2)}) copy-start(bf16[128,768]{1,0:T(8,128)(2,1)} %reduce-scatter.13.cloned.1.call-done) | copy-start | bytes 589828
  227.7 113.1 %reduce-scatter.27.cloned.1.call-start = ((), (), s32[]{:S(2)}) async-start(), calls=%async_computation.15 | async-start | bytes 1327104
  231.6 174.1 %reduce-scatter.25.cloned.1.call-start = ((), (), s32[]{:S(2)}) async-start(), calls=%async_computation.14 | async-start | bytes 884736
  275.1 12.6 %copy-start.18 = (bf16[192,768]{0,1:T(8,128)(2,1)S(1)}, bf16[192,768]{0,1:T(8,128)(2,1)}, u32[]{:S(2)}) copy-start(bf16[192,768]{0,1:T(8,128)(2,1)} %all_gather.39) | copy-start | bytes 884740
  275.1 13.0 %copy-start.30 = (bf16[3,64,512]{2,1,0:T(8,128)(2,1)S(1)}, bf16[3,64,512]{2,1,0:T(8,128)(2,1)}, u32[]{:S(2)}) copy-start(bf16[3,64,512]{2,1,0:T(8,128)(2,1)} %copy-done.29) | copy-start | bytes 589828
  294.6 137.7 %reduce-scatter.19.cloned.1.call-start = ((), (), s32[]{:S(2)}) async-start(), calls=%async_computation.11 | async-start | bytes 983040 | tf_op jit(solution)/shard_map/reduce_scatter | solution.py:76
  300.7 202.1 %reduce-scatter.23.cloned.1.call-start = ((), (), s32[]{:S(2)}) async-start(), calls=%async_computation.13 | async-start | bytes 2654208 | tf_op jit(solution)/shard_map/reduce_scatter | solution.py:254
  303.1 272.2 %reduce-scatter.21.cloned.1.call-start = ((), (), s32[]{:S(2)}) async-start(), calls=%async_computation.12 | async-start | bytes 2654208 | tf_op jit(solution)/shard_map/reduce_scatter | solution.py:252
  305.4 127.0 %copy-start.44 = (f32[128]{0:T(128)S(1)}, f32[128]{0:T(128)}, u32[]{:S(2)}) copy-start(f32[128]{0:T(128)} %copy-done.43) | copy-start | bytes 1540
  305.4 128.1 %copy-start.53 = (f32[128]{0:T(128)S(1)}, f32[128]{0:T(128)}, u32[]{:S(2)}) copy-start(f32[128]{0:T(128)} %copy-done.52) | copy-start | bytes 1540
  305.4 128.1 %copy-start.50 = (f32[128]{0:T(128)S(1)}, f32[128]{0:T(128)}, u32[]{:S(2)}) copy-start(f32[128]{0:T(128)} %copy-done.49) | copy-start | bytes 1540
  305.4 129.4 %copy-start.42 = (f32[768]{0:T(1024)S(1)}, f32[768]{0:T(1024)}, u32[]{:S(2)}) copy-start(f32[768]{0:T(1024)} %get-tuple-element.97) | copy-start | bytes 9220
  305.4 151.2 %copy-start.20 = (f32[128,768]{1,0:T(8,128)S(1)}, f32[128,768]{1,0:T(8,128)}, u32[]{:S(2)}) copy-start(f32[128,768]{1,0:T(8,128)} %copy-done.19) | copy-start | bytes 1179652
  305.4 151.2 %copy-start.23 = (bf16[128,768]{1,0:T(8,128)(2,1)S(1)}, bf16[128,768]{1,0:T(8,128)(2,1)}, u32[]{:S(2)}) copy-start(bf16[128,768]{1,0:T(8,128)(2,1)} %param.17) | copy-start | bytes 589828
  305.4 151.2 %copy-start.46 = (f32[128]{0:T(128)S(1)}, f32[128]{0:T(128)}, u32[]{:S(2)}) copy-start(f32[128]{0:T(128)} %copy-done.45) | copy-start | bytes 1540
  (31 other events, 42.9 us)
Sparse Core Ops, SparseCore 0:
  122.2 26.2 reduce-scatter.12
  222.8 26.3 reduce-scatter.16
  251.8 23.2 reduce-scatter.14
  278.7 62.0 reduce-scatter.26
  344.3 61.4 reduce-scatter.24
  408.1 24.1 reduce-scatter.18
  436.2 66.5 reduce-scatter.22
  507.3 67.9 reduce-scatter.20
where the time goes:
time: 587 us; the launch traced here: 582 us
  waiting for transfers between devices  278 us (47%)
  blocking collectives  211 us (36%)
  other arithmetic  27.2 us (5%)
  matrix products  26.3 us (4%)
  local copies, waits for them, and re-layouts  22.8 us (4%)
  between operations  16.3 us (3%)
    unnamed x10, waiting for transfers between devices  98.1 us
    reduce_scatter x1, waiting for transfers between devices, shards(): lax.psum_scatter(wqkv_grad, 'dp', scatter_dimension=0, tiled=True)  70.5 us
    reduce_scatter x4, waiting for transfers between devices, sum_rows(): lax.psum_scatter(array_in.astype(jnp.bfloat16), 'tensor', scatter_dimensi...  65.4 us
    all_gather x4, blocking collectives, gather_rows(): return lax.all_gather(array_in, 'tensor', axis=0, tiled=True)  58.6 us
    reduce_scatter x1, waiting for transfers between devices, shards(): lax.psum_scatter(wi_grad, 'dp', scatter_dimension=0, tiled=True)  44.4 us
    all_gather x1, blocking collectives, shards(): lax.all_gather(wqkv, 'dp', axis=0, tiled=True)  38.5 us
    all_gather x1, blocking collectives, shards(): lax.all_gather(wi, 'dp', axis=0, tiled=True)  28 us
    all_gather x1, blocking collectives, shards(): lax.all_gather(wo, 'dp', axis=1, tiled=True)  27.1 us
  transfers between devices with their start and end apart: 8, of which 7 were waited for; matrix products, arithmetic and copies ran while one was open for 8% of the time, Pallas kernels for 0%

commit v1 on v0

v1 whole, which is shorter than its diff:
```python
import functools

import jax
import jax.numpy as jnp
from jax import lax
from jax.experimental import pallas as pl
from jax.experimental.pallas import tpu as pltpu
from jax.sharding import PartitionSpec as P

HEAD_DIM = 64
SEQS = 2
NORM_EPS = 1e-05
ROPE_THETA = 160000.0
SCORE_SCALE = 0.125
MESH = pl.DeviceIdType.MESH
GAIN_ROWS = 16


def layout(lengths, row_count):
    seq_ends = jnp.cumsum(lengths)
    row_ids = jnp.arange(row_count, dtype=jnp.int32)
    segment = jnp.sum((row_ids[None, :] >= seq_ends[:, None]).astype(jnp.int32), axis=0)
    starts = jnp.concatenate([seq_ends - lengths, seq_ends[-1:]])
    slot_ids = jnp.arange(lengths.shape[0] + 1, dtype=jnp.int32)
    seq_begin = jnp.sum(
        jnp.where(segment[None, :] == slot_ids[:, None], starts[:, None], 0), axis=0
    )
    return (segment, row_ids - seq_begin)


def unit_rows(array_in):
    row_mean = jnp.mean(array_in, axis=-1, keepdims=True)
    centred = array_in - row_mean
    spread = jnp.mean(centred * centred, axis=-1, keepdims=True)
    inverse = lax.rsqrt(spread + NORM_EPS)
    return centred * inverse, inverse


def norm_back(unit, inverse, gain, grad):
    pulled = grad * gain
    mean_pull = jnp.mean(pulled, axis=-1, keepdims=True)
    mean_both = jnp.mean(pulled * unit, axis=-1, keepdims=True)
    return (pulled - mean_pull - unit * mean_both) * inverse


def rotation(position):
    half_dim = HEAD_DIM // 2
    frequency = ROPE_THETA ** (-jnp.arange(half_dim, dtype=jnp.float32) / half_dim)
    angles = position.astype(jnp.float32)[:, None] * frequency[None, :]
    return (jnp.cos(angles)[:, None, :], jnp.sin(angles)[:, None, :])


def rotate(array_in, cosine, sine_table):
    half_dim = HEAD_DIM // 2
    first_half = array_in[..., :half_dim]
    second_half = array_in[..., half_dim:]
    return jnp.concatenate(
        [
            first_half * cosine - second_half * sine_table,
            second_half * cosine + first_half * sine_table,
        ],
        axis=-1,
    )


def places(n_dp, n_t):
    me = lax.axis_index("dp")
    rank = lax.axis_index("tensor")
    return me, rank


def greet(n_dp, n_t, me, rank):
    barrier = pltpu.get_barrier_semaphore()
    for step in range(1, n_t):
        pl.semaphore_signal(
            barrier, inc=1, device_id={"tensor": lax.rem(rank + step, n_t)}, device_id_type=MESH
        )
    for step in range(1, n_dp):
        pl.semaphore_signal(
            barrier, inc=1, device_id={"dp": lax.rem(me + step, n_dp)}, device_id_type=MESH
        )
    pl.semaphore_wait(barrier, n_dp + n_t - 2)


def send(src, dst, send_sem, recv_sem, device):
    copy = pltpu.make_async_remote_copy(
        src_ref=src,
        dst_ref=dst,
        send_sem=send_sem,
        recv_sem=recv_sem,
        device_id=device,
        device_id_type=MESH,
    )
    copy.start()
    return copy


class DpGather:
    def __init__(self, n_dp, me, own, full, sems):
        self.n_outer = n_dp // 2
        self.full, self.sems = full, sems
        self.outer, self.inner = lax.div(me, 2), lax.rem(me, 2)
        self.partner = {"dp": me + 1 - 2 * self.inner}
        full[me] = own[...]
        self.first, self.second = [], []
        for step in range(1, self.n_outer):
            peer = lax.rem(self.outer + step, self.n_outer) * 2 + self.inner
            self.first.append(
                send(full.at[me], full.at[me], sems.at[0, step], sems.at[1, step], {"dp": peer})
            )
        self.second.append(
            send(full.at[me], full.at[me], sems.at[2, 0], sems.at[3, 0], self.partner)
        )

    def forward(self):
        for step in range(1, self.n_outer):
            self.first[step - 1].wait_recv()
            source = lax.rem(self.outer + self.n_outer - step, self.n_outer) * 2 + self.inner
            self.second.append(
                send(
                    self.full.at[source],
                    self.full.at[source],
                    self.sems.at[2, step],
                    self.sems.at[3, step],
                    self.partner,
                )
            )

    def finish(self):
        for copy in self.second:
            copy.wait_recv()
        for copy in self.first + self.second:
            copy.wait_send()


class DpReduce:
    def __init__(self, n_dp, me, parts, pair, sums, far, sems):
        self.n_outer = n_dp // 2
        self.me, self.parts, self.pair, self.sums, self.far, self.sems = (
            me, parts, pair, sums, far, sems,
        )
        self.outer, self.inner = lax.div(me, 2), lax.rem(me, 2)
        partner = {"dp": me + 1 - 2 * self.inner}
        self.first, self.second = {}, {}
        for step in list(range(1, self.n_outer)) + [0]:
            block = lax.rem(self.outer + step, self.n_outer) * 2 + 1 - self.inner
            self.first[step] = send(
                parts.at[block], pair.at[step], sems.at[0, step], sems.at[1, step], partner
            )

    def forward(self):
        for step in range(1, self.n_outer):
            self.first[step].wait_recv()
            peer = lax.rem(self.outer + step, self.n_outer) * 2 + self.inner
            self.sums[step] = (
                self.parts[peer].astype(jnp.float32) + self.pair[step].astype(jnp.float32)
            ).astype(jnp.bfloat16)
            self.second[step] = send(
                self.sums.at[step],
                self.far.at[step],
                self.sems.at[2, step],
                self.sems.at[3, step],
                {"dp": peer},
            )

    def finish(self, out):
        self.first[0].wait_recv()
        total = self.parts[self.me].astype(jnp.float32) + self.pair[0].astype(jnp.float32)
        for step in range(1, self.n_outer):
            self.second[step].wait_recv()
            total = total + self.far[step].astype(jnp.float32)
        out[...] = total
        for copy in list(self.first.values()) + list(self.second.values()):
            copy.wait_send()


def start_rows_sum(n_t, rank, parts, slots, sems):
    copies = []
    for step in range(1, n_t):
        peer = lax.rem(rank + step, n_t)
        copies.append(
            send(parts.at[peer], slots.at[step - 1], sems.at[0, step], sems.at[1, step],
                 {"tensor": peer})
        )
    return copies


def end_rows_sum(n_t, rank, parts, slots, copies):
    total = parts[rank].astype(jnp.float32)
    for step in range(1, n_t):
        copies[step - 1].wait_recv()
        total = total + slots[step - 1].astype(jnp.float32)
    return total


def start_rows_gather(n_t, rank, full, sems):
    return [
        send(full.at[rank], full.at[rank], sems.at[0, step], sems.at[1, step],
             {"tensor": lax.rem(rank + step, n_t)})
        for step in range(1, n_t)
    ]


def end_sends(copies):
    for copy in copies:
        copy.wait_send()


def end_all(copies):
    for copy in copies:
        copy.wait_recv()
    end_sends(copies)


def gather_kernel(n_dp, n_t, w_ref, x_ref, cot_ref, w_all, x_all, cot_all, w_sems, x_sems, cot_sems):
    me, rank = places(n_dp, n_t)
    x_all[rank] = x_ref[...]
    cot_all[rank] = cot_ref[...]
    greet(n_dp, n_t, me, rank)
    weights = DpGather(n_dp, me, w_ref, w_all, w_sems)
    x_copies = start_rows_gather(n_t, rank, x_all, x_sems)
    cot_copies = start_rows_gather(n_t, rank, cot_all, cot_sems)
    weights.forward()
    end_all(x_copies)
    end_all(cot_copies)
    weights.finish()


def middle_kernel(
    n_dp, n_t, w_ref, part_ref, x_ref, gain_ref, w_all, residual_ref, mlp_all,
    slots, w_sems, part_sems, row_sems,
):
    me, rank = places(n_dp, n_t)
    greet(n_dp, n_t, me, rank)
    part_copies = start_rows_sum(n_t, rank, part_ref, slots, part_sems)
    weights = DpGather(n_dp, me, w_ref, w_all, w_sems)
    total = end_rows_sum(n_t, rank, part_ref, slots, part_copies)
    residual = x_ref[...].astype(jnp.float32) + total
    residual_ref[...] = residual
    unit, unused_inverse = unit_rows(residual)
    mlp_all[rank] = (unit * gain_ref[...]).astype(jnp.bfloat16)
    row_copies = start_rows_gather(n_t, rank, mlp_all, row_sems)
    weights.forward()
    end_all(row_copies)
    end_sends(part_copies)
    weights.finish()


def turn_kernel(
    n_dp, n_t, grads_ref, back_ref, out_part_ref, residual_ref, gain_ref, cot_ref, valid_ref,
    w_sum, output_ref, grad_residual_ref, grad_all, gain_part,
    back_slots, out_slots, pair, sums, far, back_sems, out_sems, w_sems, row_sems,
):
    me, rank = places(n_dp, n_t)
    greet(n_dp, n_t, me, rank)
    back_copies = start_rows_sum(n_t, rank, back_ref, back_slots, back_sems)
    weights = DpReduce(n_dp, me, grads_ref, pair, sums, far, w_sems)
    grad = end_rows_sum(n_t, rank, back_ref, back_slots, back_copies)
    residual = residual_ref[...]
    valid = valid_ref[...]
    unit, inverse = unit_rows(residual)
    gain_part[...] = jnp.sum(grad * unit, axis=0, keepdims=True)
    grad_residual = valid * cot_ref[...].astype(jnp.float32) + norm_back(
        unit, inverse, gain_ref[...], grad
    )
    grad_residual_ref[...] = grad_residual
    grad_all[rank] = grad_residual.astype(jnp.bfloat16)
    row_copies = start_rows_gather(n_t, rank, grad_all, row_sems)
    out_copies = start_rows_sum(n_t, rank, out_part_ref, out_slots, out_sems)
    weights.forward()
    end_all(row_copies)
    mlp_out = end_rows_sum(n_t, rank, out_part_ref, out_slots, out_copies)
    output_ref[...] = (valid * (residual + mlp_out)).astype(jnp.bfloat16)
    end_sends(back_copies)
    end_sends(out_copies)
    weights.finish(w_sum)


def last_kernel(
    n_dp, n_t, grads_ref, back_ref, x_ref, gain_ref, grad_residual_ref, gain_part_ref,
    w_sum, input_grad_ref, gain_sum_ref,
    back_slots, pair, sums, far, own_gain, near_gain, group_gain, far_gain,
    back_sems, w_sems, near_sems, far_sems,
):
    me, rank = places(n_dp, n_t)
    greet(n_dp, n_t, me, rank)
    back_copies = start_rows_sum(n_t, rank, back_ref, back_slots, back_sems)
    weights = DpReduce(n_dp, me, grads_ref, pair, sums, far, w_sems)
    grad = end_rows_sum(n_t, rank, back_ref, back_slots, back_copies)
    unit, inverse = unit_rows(x_ref[...].astype(jnp.float32))
    width = unit.shape[1]
    own_gain[0:1, :] = jnp.sum(grad * unit, axis=0, keepdims=True)
    own_gain[1:2, :] = gain_part_ref[...]
    own_gain[2:8, :] = jnp.zeros((6, width), jnp.float32)
    near = [
        send(own_gain, near_gain.at[step - 1], near_sems.at[0, step], near_sems.at[1, step],
             {"tensor": lax.rem(rank + step, n_t)})
        for step in range(1, n_t)
    ]
    input_grad_ref[...] = (
        grad_residual_ref[...] + norm_back(unit, inverse, gain_ref[...], grad)
    ).astype(jnp.bfloat16)
    total = own_gain[...]
    for step in range(1, n_t):
        near[step - 1].wait_recv()
        total = total + near_gain[step - 1]
    group_gain[...] = total
    far_copies = [
        send(group_gain, far_gain.at[step - 1], far_sems.at[0, step], far_sems.at[1, step],
             {"dp": lax.rem(me + step, n_dp)})
        for step in range(1, n_dp)
    ]
    weights.forward()
    for step in range(1, n_dp):
        far_copies[step - 1].wait_recv()
        total = total + far_gain[step - 1]
    gain_sum_ref[...] = total
    end_sends(near)
    end_sends(far_copies)
    end_sends(back_copies)
    weights.finish(w_sum)


def call(kernel, n_dp, n_t, number, outs, scratch, operands):
    in_vmem = pl.BlockSpec(memory_space=pltpu.VMEM)
    moved = sum(op.size * op.dtype.itemsize for op in operands)
    return pl.pallas_call(
        functools.partial(kernel, n_dp, n_t),
        out_shape=[jax.ShapeDtypeStruct(shape, kind) for shape, kind in outs],
        in_specs=[in_vmem] * len(operands),
        out_specs=[in_vmem] * len(outs),
        scratch_shapes=scratch,
        compiler_params=pltpu.CompilerParams(
            collective_id=number, has_side_effects=True, vmem_limit_bytes=40 * 2**20
        ),
        cost_estimate=pl.CostEstimate(flops=0, bytes_accessed=2 * moved, transcendentals=0),
    )(*operands)


def dot(first, second, dims):
    return lax.dot_general(first, second, (dims, ((), ())), preferred_element_type=jnp.float32)


def shards(inputs, seq_lengths, attn_gain, wqkv, wo, mlp_gain, wi, wo2, cotangent):
    low = jnp.bfloat16
    n_dp, n_t = lax.axis_size("dp"), lax.axis_size("tensor")
    me, rank = lax.axis_index("dp"), lax.axis_index("tensor")
    local_rows, width = inputs.shape
    group_rows = local_rows * n_t
    depth = wqkv.shape[0]
    head_cols = wqkv.shape[2]
    heads_here = head_cols // HEAD_DIM
    hidden_cols = wi.shape[2]
    first_cols = 3 * head_cols + wo.shape[0]
    second_cols = 2 * hidden_cols + wo2.shape[0]
    n_outer = n_dp // 2

    def dma(count):
        return pltpu.SemaphoreType.DMA(count)

    def row_sems():
        return dma((2, n_t))

    segment, position = layout(seq_lengths[0], group_rows)
    valid_all = (segment < SEQS).astype(jnp.float32)[:, None]
    valid_rows = lax.dynamic_slice_in_dim(valid_all, rank * local_rows, local_rows)
    cosine, sine_table = rotation(position)

    gain_row = jnp.concatenate([attn_gain, mlp_gain])
    gain_block = jnp.zeros((GAIN_ROWS, first_cols), low).at[0, : 2 * depth].set(gain_row)
    first_block = jnp.concatenate(
        [jnp.concatenate([wqkv.reshape(depth, 3 * head_cols), wo.T], axis=1), gain_block], axis=0
    )
    second_block = jnp.concatenate([wi.reshape(depth, 2 * hidden_cols), wo2.T], axis=1)

    first_all, x_all, cot_all = call(
        gather_kernel, n_dp, n_t, 1,
        [
            ((n_dp,) + first_block.shape, low),
            ((n_t, local_rows, width), low),
            ((n_t, local_rows, width), low),
        ],
        [dma((4, n_outer)), row_sems(), row_sems()],
        (first_block, inputs, cotangent),
    )
    full_qkv = first_all[:, :depth, : 3 * head_cols].reshape(width, 3 * head_cols)
    full_wo = first_all[:, :depth, 3 * head_cols :].reshape(width, wo.shape[0])
    gain_one = first_all[:, depth, :depth].reshape(1, width).astype(jnp.float32)
    gain_two = first_all[:, depth, depth : 2 * depth].reshape(1, width).astype(jnp.float32)
    grad_mlp_all = (
        valid_all * cot_all.reshape(group_rows, width).astype(jnp.float32)
    ).astype(low)

    unit, unused_inverse = unit_rows(x_all.reshape(group_rows, width).astype(jnp.float32))
    attn_all = (unit * gain_one).astype(low)
    qkv = dot(attn_all, full_qkv, ((1,), (0,))).reshape(group_rows, 3, heads_here, HEAD_DIM)
    query_low = rotate(qkv[:, 0], cosine, sine_table).astype(low)
    key_low = rotate(qkv[:, 1], cosine, sine_table).astype(low)
    value_low = qkv[:, 2].astype(low)
    scores = (
        jnp.einsum("qhd,khd->hqk", query_low, key_low, preferred_element_type=jnp.float32)
        * SCORE_SCALE
    )
    scores = jnp.where((segment[:, None] == segment[None, :])[None], scores, -1e30)
    exponent = jnp.exp(scores - jnp.max(scores, axis=-1, keepdims=True))
    probs = exponent / jnp.sum(exponent, axis=-1, keepdims=True)
    prob_low = probs.astype(low)
    context = (
        jnp.einsum("hqk,khd->qhd", prob_low, value_low, preferred_element_type=jnp.float32)
        .astype(low)
        .reshape(group_rows, head_cols)
    )
    attn_part = dot(context, full_wo, ((1,), (1,))).astype(low)

    row_block = (n_t, local_rows, width)
    slots = pltpu.VMEM((n_t - 1, local_rows, width), low)
    second_all, residual, mlp_all = call(
        middle_kernel, n_dp, n_t, 2,
        [
            ((n_dp,) + second_block.shape, low),
            ((local_rows, width), jnp.float32),
            (row_block, low),
        ],
        [slots, dma((4, n_outer)), row_sems(), row_sems()],
        (second_block, attn_part.reshape(row_block), inputs, gain_two),
    )
    full_wi = second_all[:, :, : 2 * hidden_cols].reshape(width, 2 * hidden_cols)
    full_wo2 = second_all[:, :, 2 * hidden_cols :].reshape(width, wo2.shape[0])
    mlp_all = mlp_all.reshape(group_rows, width)
    projected = dot(mlp_all, full_wi, ((1,), (0,)))
    gate, other = projected[:, :hidden_cols], projected[:, hidden_cols:]
    bell = 0.5 * (1.0 + lax.erf(gate * 0.7071067811865476))
    gelu = gate * bell
    slope = bell + gate * jnp.exp(-0.5 * gate * gate) * 0.3989422804014327
    hidden = (gelu * other).astype(low)
    out_part = dot(hidden, full_wo2, ((1,), (1,))).astype(low)
    grad_hidden = dot(grad_mlp_all, full_wo2, ((1,), (0,)))
    grad_proj = jnp.concatenate(
        [grad_hidden * other * slope, grad_hidden * gelu], axis=1
    ).astype(low)
    back_part = dot(grad_proj, full_wi, ((1,), (1,))).astype(low)
    second_grads = jnp.concatenate(
        [
            dot(mlp_all, grad_proj, ((0,), (0,))).astype(low),
            dot(grad_mlp_all, hidden, ((0,), (0,))).astype(low),
        ],
        axis=1,
    ).reshape(n_dp, depth, second_cols)

    def reduce_scratch(cols):
        return [pltpu.VMEM((n_outer, depth, cols), low)] * 3

    second_sum, output, grad_residual, grad_all, gain_part = call(
        turn_kernel, n_dp, n_t, 3,
        [
            ((depth, second_cols), jnp.float32),
            ((local_rows, width), low),
            ((local_rows, width), jnp.float32),
            (row_block, low),
            ((1, width), jnp.float32),
        ],
        [slots, slots] + reduce_scratch(second_cols)
        + [row_sems(), row_sems(), dma((4, n_outer)), row_sems()],
        (
            second_grads, back_part.reshape(row_block), out_part.reshape(row_block),
            residual, gain_two, cotangent, valid_rows,
        ),
    )
    grad_all = grad_all.reshape(group_rows, width)
    grad_context = dot(grad_all, full_wo, ((1,), (0,))).astype(low)
    grad_context = grad_context.reshape(group_rows, heads_here, HEAD_DIM)
    grad_value = jnp.einsum(
        "hqk,qhd->khd", prob_low, grad_context, preferred_element_type=jnp.float32
    )
    grad_probs = jnp.einsum(
        "qhd,khd->hqk", grad_context, value_low, preferred_element_type=jnp.float32
    )
    row_inner = jnp.sum(probs * grad_probs, axis=-1, keepdims=True)
    grad_scores = (probs * (grad_probs - row_inner)).astype(low)
    grad_query = (
        jnp.einsum("hqk,khd->qhd", grad_scores, key_low, preferred_element_type=jnp.float32)
        * SCORE_SCALE
    )
    grad_key = (
        jnp.einsum("hqk,qhd->khd", grad_scores, query_low, preferred_element_type=jnp.float32)
        * SCORE_SCALE
    )
    grad_qkv = jnp.stack(
        [
            rotate(grad_query, cosine, -sine_table),
            rotate(grad_key, cosine, -sine_table),
            grad_value,
        ],
        axis=1,
    )
    grad_qkv = grad_qkv.astype(low).reshape(group_rows, 3 * head_cols)
    first_grads = jnp.concatenate(
        [
            dot(attn_all, grad_qkv, ((0,), (0,))).astype(low),
            dot(grad_all, context, ((0,), (0,))).astype(low),
        ],
        axis=1,
    ).reshape(n_dp, depth, first_cols)
    attn_back = dot(grad_qkv, full_qkv, ((1,), (1,))).astype(low)

    gain_block_f32 = pltpu.VMEM((8, width), jnp.float32)
    first_sum, input_grad, gain_sum = call(
        last_kernel, n_dp, n_t, 4,
        [
            ((depth, first_cols), jnp.float32),
            ((local_rows, width), low),
            ((8, width), jnp.float32),
        ],
        [slots] + reduce_scratch(first_cols)
        + [
            gain_block_f32,
            pltpu.VMEM((n_t - 1, 8, width), jnp.float32),
            gain_block_f32,
            pltpu.VMEM((n_dp - 1, 8, width), jnp.float32),
            row_sems(), dma((4, n_outer)), row_sems(), dma((2, n_dp)),
        ],
        (
            first_grads, attn_back.reshape(row_block), inputs, gain_one, grad_residual, gain_part,
        ),
    )
    gains_here = lax.dynamic_slice_in_dim(gain_sum[:2], me * depth, depth, axis=1)
    return (
        output,
        input_grad,
        gains_here[0],
        first_sum[:, : 3 * head_cols].reshape(depth, 3, head_cols),
        first_sum[:, 3 * head_cols :].T,
        gains_here[1],
        second_sum[:, : 2 * hidden_cols].reshape(depth, 2, hidden_cols),
        second_sum[:, 2 * hidden_cols :].T,
    )


def solution(mesh):
    in_specs = (
        P(("dp", "tensor"), None),
        P("dp", None),
        P("dp"),
        P("dp", None, "tensor"),
        P("tensor", "dp"),
        P("dp"),
        P("dp", None, "tensor"),
        P("tensor", "dp"),
        P(("dp", "tensor"), None),
    )
    out_specs = (
        P(("dp", "tensor"), None),
        P(("dp", "tensor"), None),
        P("dp"),
        P("dp", None, "tensor"),
        P("tensor", "dp"),
        P("dp"),
        P("dp", None, "tensor"),
        P("tensor", "dp"),
    )
    return jax.shard_map(shards, mesh=mesh, in_specs=in_specs, out_specs=out_specs, check_vma=False)
```

time: 587 us -> 172 us (0.29)
  waiting for transfers between devices: 278 us -> 0 us
  blocking collectives: 211 us -> 0 us
  Pallas kernels: 0 us -> 115 us
  between operations: 16.3 us -> 1.22 us
  other arithmetic: 27.2 us -> 12.7 us
  matrix products: 26.3 us -> 19.9 us
    reduce_scatter x6 -> x0, waiting for transfers between devices: 180 us -> none  [the longest x1 70.5 us: shards(): lax.psum_scatter(wqkv_grad, 'dp', scatter_dimension=0, tiled=True)]
    all_gather x8 -> x0, blocking collectives: 177 us -> none  [the longest x4 58.6 us: gather_rows(): return lax.all_gather(array_in, 'tensor', axis=0, tiled=True)]
    pallas_call x0 -> x4, Pallas kernels: none -> 115 us  [call(): pl.pallas_call(functools.partial(kernel, n_dp, n_t), out_shape=[jax.Shape...]
    unnamed x10 -> x0, waiting for transfers between devices: 98.1 us -> none
    unnamed x2 -> x0, blocking collectives: 24.3 us -> none
    psum x1 -> x0, blocking collectives: 9.56 us -> none  [shards(): lax.psum((attn_gain_part, mlp_gain_part), 'tensor')]
    reduce_sum x9 -> x2, other arithmetic: 11 us -> 1.52 us  [the longest x1 1.15 us: unit_rows(): row_mean = jnp.mean(array_in, axis=-1, keepdims=True)]
    unnamed x124 -> x62, local copies, waits for them, and re-layouts: 19.1 us -> 10.9 us
  transfers between devices with their start and end apart: 8 -> 0, of which waited for: 7 -> 0; matrix products, arithmetic and copies ran while one was open for 8% -> 0% of each run, Pallas kernels for 0% -> 0%
where the time goes in v1:
time: 172 us; the launch traced here: 171 us
  Pallas kernels  115 us (67%)
  local copies, waits for them, and re-layouts  22.3 us (13%)
  matrix products  19.9 us (12%)
  other arithmetic  12.7 us (7%)
    pallas_call x4, Pallas kernels, call(): pl.pallas_call(functools.partial(kernel, n_dp, n_t), out_shape=[jax.Shape...  115 us
    unnamed x62, local copies, waits for them, and re-layouts  10.9 us
    dot_general x12, matrix products, dot(): lax.dot_general(first, second, (dims, ((), ())), preferred_element_type=j...  9.33 us

profile of v1, /device:TPU:11, one launch (start us, length us, event | category | flops | bytes accessed | tf_op | source)
XLA Modules:
  0.0 171.0 jit_solution(1645070927442158480)
XLA Ops:
  0.7 0.9 broadcast_in_dim.24
  4.5 0.9 copy.49
  6.2 1.0 copy.47
  7.1 1.1 reshape.344
  8.3 1.1 copy.48
  9.6 1.0 fusion.31
  10.6 0.9 broadcast_compare_fusion
  11.5 23.2 %shard_map.152 = (bf16[8,112,768]{2,1,0:T(8,128)(2,1)S(1)}, bf16[4,128,768]{2,1,0:T(8,128)(2,1)S(1)}, bf16[4,128,768]{2,1,0:T(8,128)(2,1)S(1)}) custom-call(bf16[112,768]{1,0:T(8,128)(2,1)S(1)} %fusion.26.w_ref, bf16[128,768]{1,0:T(8,128)(2,1)S(1)} %copy-done, bf16[128,768]{1,0:T(8,128)(2,1)S(1)} %copy-done.1), custom_call_target="tpu_custom_call" | custom-call | bytes 1130496 | tf_op jit(solution)/shard_map/pallas_call | solution.py:327
  35.1 1.0 slice.112
  36.1 1.1 slice.102
  37.1 1.1 fusion.7
  38.2 1.1 convert_reduce_fusion
  39.8 1.2 fusion.6
  41.6 1.8 %fusion.46 = f32[512,3,3,64]{0,3,2,1:T(8,128)S(1)} fusion(bf16[512,768,1,1]{1,0,3,2:T(8,128)(2,1)} %bitcast.118, bf16[3,3,64,768]{3,2,1,0:T(8,128)(2,1)S(1)} %bitcast.115), kind=kOutput, calls=%fused_computation.111 | convolution fusion | flops 452984832 | bytes 2850816 | tf_op jit(solution)/shard_map/dot_general | solution.py:341
  43.7 0.8 copy-done.26
  44.6 2.9 %fusion.45 = (f32[3,512]{1,0:T(4,128)S(1)}, f32[3,512,512]{1,2,0:T(8,128)}) fusion(pred[512,512]{0,1:T(8,128)(4,1)S(1)} %copy-done.26, bf16[512,3,32]{0,2,1:T(8,128)(2,1)S(1)} %get-tuple-element.89, bf16[512,3,32]{0,2,1:T(8,128)(2,1)S(1)} %get-tuple-element.90, bf16[512,3,32]{0,2,1:T(8,128)(2,1)S(1)} %get-tuple-element.84, ...), kind=kOutput, calls=%fused_computation.110 | convolution fusion | flops 104595968 | bytes 3807232 | tf_op jit(solution)/shard_map/sub | solution.py:405
  47.6 2.4 %convolution_convert_fusion.10 = bf16[3,64,512]{2,1,0:T(8,128)(2,1)S(1)} fusion(f32[512,3,3,64]{0,3,2,1:T(8,128)S(1)} %fusion.46, f32[3,512,512]{1,2,0:T(8,128)} %get-tuple-element.99, f32[3,512]{1,0:T(4,128)S(1)} %get-tuple-element.98), kind=kOutput, calls=%fused_computation.36 | convolution fusion | flops 102334464 | bytes 3547136 | tf_op jit(solution)/shard_map/hqk,khd->qhd/dot_general | solution.py:409
  50.4 28.2 %shard_map.153 = (bf16[8,96,864]{2,1,0:T(8,128)(2,1)S(1)}, f32[128,768]{1,0:T(8,128)S(1)}, bf16[4,128,768]{2,1,0:T(8,128)(2,1)S(1)}) custom-call(bf16[96,864]{1,0:T(8,128)(2,1)S(1)} %pad_maximum_fusion.8.w_ref, bf16[4,128,768]{2,1,0:T(8,128)(2,1)S(1)} %bitcast.105, bf16[128,768]{1,0:T(8,128)(2,1)S(1)} %copy-done, f32[1,768]{1,0:T(1,128)S(1)} %reshape.365.gain_ref), custom_call_target="tpu_custom_call" | custom-call | bytes 2304000 | tf_op jit(solution)/shard_map/pallas_call | solution.py:327
  82.0 0.8 convolution_convert_fusion.3
  83.5 1.2 pad_maximum_fusion
  84.6 2.0 %copy.53 = bf16[768,864]{1,0:T(8,128)(2,1)S(1)} copy(bf16[768,864]{0,1:T(8,128)(2,1)} %pad_maximum_fusion) | data formatting | bytes 2654208 | tf_op jit(solution)/shard_map/concatenate | solution.py:442
  86.6 1.7 %convolution_convert_fusion.5 = bf16[512,768]{1,0:T(8,128)(2,1)S(1)} fusion(bf16[512,288]{0,1:T(8,128)(2,1)S(1)} %get-tuple-element.76, bf16[768,288]{1,0:T(8,128)(2,1)} %bitcast.121), kind=kOutput, calls=%fused_computation.25 | convolution fusion | flops 226885632 | bytes 1523712 | tf_op jit(solution)/shard_map/dot_general | solution.py:341
  88.4 29.7 %shard_map.154 = (f32[96,864]{1,0:T(8,128)S(1)}, bf16[128,768]{1,0:T(8,128)(2,1)S(1)}, f32[128,768]{1,0:T(8,128)S(1)}, bf16[4,128,768]{2,1,0:T(8,128)(2,1)S(1)}, f32[1,768]{1,0:T(1,128)S(1)}) custom-call(bf16[8,96,864]{2,1,0:T(8,128)(2,1)S(1)} %bitcast.101, bf16[4,128,768]{2,1,0:T(8,128)(2,1)S(1)} %bitcast.110, bf16[4,128,768]{2,1,0:T(8,128)(2,1)S(1)} %bitcast.106, ...), custom_call_target="tpu_custom_call" | custom-call | bytes 6986752 | tf_op jit(solution)/shard_map/pallas_call | solution.py:327
  119.8 0.9 reshape.363
  120.7 2.6 %fusion.13 = bf16[512,1,3,64]{0,3,2,1:T(8,128)(2,1)S(1)} fusion(bf16[512,3,64]{0,2,1:T(8,128)(2,1)S(1)} %bitcast.131, f32[3,512,512]{1,2,0:T(8,128)} %get-tuple-element.99, f32[3,512]{1,0:T(4,128)S(1)} %get-tuple-element.98), kind=kOutput, calls=%fused_computation.37 | convolution fusion | flops 102334464 | bytes 3545088 | tf_op jit(solution)/shard_map/hqk,qhd->khd/dot_general | solution.py:472
  123.5 1.6 multiply_reduce_fusion
  125.2 0.9 multiply_convert_fusion
  128.2 0.9 copy-done.6
  130.6 1.1 pad_maximum_fusion.1
  131.7 1.6 copy.58
  133.3 33.9 %shard_map.155 = (f32[96,768]{1,0:T(8,128)S(1)}, bf16[128,768]{1,0:T(8,128)(2,1)S(1)}, f32[8,768]{1,0:T(8,128)S(1)}) custom-call(bf16[8,96,768]{2,1,0:T(8,128)(2,1)S(1)} %bitcast.102, bf16[4,128,768]{2,1,0:T(8,128)(2,1)S(1)} %bitcast.109, bf16[128,768]{1,0:T(8,128)(2,1)S(1)} %copy-done, f32[1,768]{1,0:T(1,128)S(1)} %reshape.368.gain_ref, ...), custom_call_target="tpu_custom_call" | custom-call | bytes 5124096 | tf_op jit(solution)/shard_map/pallas_call | solution.py:327
  168.8 0.9 copy.60
  (107 shorter events, 18.3 us)
Async XLA Ops:
  0.6 10.9 %copy-start = (bf16[128,768]{1,0:T(8,128)(2,1)S(1)}, bf16[128,768]{1,0:T(8,128)(2,1)}, u32[]{:S(2)}) copy-start(bf16[128,768]{1,0:T(8,128)(2,1)} %x_ref.5) | copy-start | bytes 589828
  0.6 10.9 %copy-start.1 = (bf16[128,768]{1,0:T(8,128)(2,1)S(1)}, bf16[128,768]{1,0:T(8,128)(2,1)}, u32[]{:S(2)}) copy-start(bf16[128,768]{1,0:T(8,128)(2,1)} %cot_ref.3) | copy-start | bytes 589828
  39.4 1.6 copy-start.5
  41.6 2.0 %copy-start.15 = (f32[512,32]{0,1:T(8,128)S(1)}, f32[512,32]{0,1:T(8,128)}, u32[]{:S(2)}) copy-start(f32[512,32]{0,1:T(8,128)} %get-tuple-element.93) | copy-start | bytes 196612
  41.6 2.0 %copy-start.25 = (f32[512,32]{0,1:T(8,128)S(1)}, f32[512,32]{0,1:T(8,128)}, u32[]{:S(2)}) copy-start(f32[512,32]{0,1:T(8,128)} %get-tuple-element.92) | copy-start | bytes 196612
  43.4 4.1 %copy-start.9 = (f32[512,3,3,64]{0,3,2,1:T(8,128)}, f32[512,3,3,64]{0,3,2,1:T(8,128)S(1)}, u32[]{:S(2)}) copy-start(f32[512,3,3,64]{0,3,2,1:T(8,128)S(1)} %fusion.46) | copy-start | bytes 3538948
  43.5 1.1 copy-start.26
  43.7 3.8 %copy-start.16 = (bf16[512,3,32]{0,2,1:T(8,128)(2,1)}, bf16[512,3,32]{0,2,1:T(8,128)(2,1)S(1)}, u32[]{:S(2)}) copy-start(bf16[512,3,32]{0,2,1:T(8,128)(2,1)S(1)} %get-tuple-element.89) | copy-start | bytes 294916
  43.7 3.8 %copy-start.18 = (bf16[512,3,32]{0,2,1:T(8,128)(2,1)}, bf16[512,3,32]{0,2,1:T(8,128)(2,1)S(1)}, u32[]{:S(2)}) copy-start(bf16[512,3,32]{0,2,1:T(8,128)(2,1)S(1)} %get-tuple-element.90) | copy-start | bytes 294916
  43.7 3.8 %copy-start.20 = (bf16[512,3,32]{0,2,1:T(8,128)(2,1)}, bf16[512,3,32]{0,2,1:T(8,128)(2,1)S(1)}, u32[]{:S(2)}) copy-start(bf16[512,3,32]{0,2,1:T(8,128)(2,1)S(1)} %get-tuple-element.83) | copy-start | bytes 294916
  43.7 3.8 %copy-start.22 = (bf16[512,3,32]{0,2,1:T(8,128)(2,1)}, bf16[512,3,32]{0,2,1:T(8,128)(2,1)S(1)}, u32[]{:S(2)}) copy-start(bf16[512,3,32]{0,2,1:T(8,128)(2,1)S(1)} %get-tuple-element.84) | copy-start | bytes 294916
  47.5 2.4 %copy-start.7 = (bf16[8,96,192]{2,1,0:T(8,128)(2,1)S(1)}, bf16[8,96,192]{2,1,0:T(8,128)(2,1)}, u32[]{:S(2)}) copy-start(bf16[8,96,192]{2,1,0:T(8,128)(2,1)} %slice.112) | copy-start | bytes 884740
  78.6 0.8 copy-start.2
  78.8 1.2 copy-start.13
  79.3 1.1 copy-start.14
  80.5 1.1 copy-start.10
  84.6 3.7 %copy-start.4 = (f32[128,1]{1,0:T(8,128)S(1)}, f32[128,1]{1,0:T(8,128)}, u32[]{:S(2)}) copy-start(f32[128,1]{1,0:T(8,128)} %copy.54.valid_ref) | copy-start | bytes 1540
  86.6 1.7 %copy-start.3 = (f32[128,768]{1,0:T(8,128)S(1)}, f32[128,768]{1,0:T(8,128)}, u32[]{:S(2)}) copy-start(f32[128,768]{1,0:T(8,128)} %copy-done.2) | copy-start | bytes 1179652
  88.4 29.7 %copy-start.8 = (bf16[8,96,192]{2,1,0:T(8,128)(2,1)S(1)}, bf16[8,96,192]{2,1,0:T(8,128)(2,1)}, u32[]{:S(2)}) copy-start(bf16[8,96,192]{2,1,0:T(8,128)(2,1)} %slice.112) | copy-start | bytes 884740
  120.7 2.8 %copy-start.12 = (f32[3,512,512]{1,2,0:T(8,128)S(1)}, f32[3,512,512]{1,2,0:T(8,128)}, u32[]{:S(2)}) copy-start(f32[3,512,512]{1,2,0:T(8,128)} %get-tuple-element.99) | copy-start | bytes 9437188
  125.2 0.9 copy-start.21
  125.2 0.9 copy-start.23
  126.1 0.9 copy-start.17
  126.1 0.9 copy-start.19
  127.1 0.8 copy-start.24
  127.9 1.2 copy-start.6
  128.2 1.8 %copy-start.11 = (bf16[4,128,768]{2,1,0:T(8,128)(2,1)S(1)}, bf16[4,128,768]{2,1,0:T(8,128)(2,1)}, u32[]{:S(2)}) copy-start(bf16[4,128,768]{2,1,0:T(8,128)(2,1)} %fusion.6) | copy-start | bytes 2359300

commit v2 on v1

--- a/solution.py
+++ b/solution.py
@@ -63,23 +63,21 @@
     )
 
 
-def places(n_dp, n_t):
-    me = lax.axis_index("dp")
-    rank = lax.axis_index("tensor")
-    return me, rank
-
-
-def greet(n_dp, n_t, me, rank):
+def flip(index):
+    return index + 1 - 2 * lax.rem(index, 2)
+
+
+def greet(n_dp, n_t, me, rank, all_dp=False):
     barrier = pltpu.get_barrier_semaphore()
-    for step in range(1, n_t):
-        pl.semaphore_signal(
-            barrier, inc=1, device_id={"tensor": lax.rem(rank + step, n_t)}, device_id_type=MESH
-        )
-    for step in range(1, n_dp):
-        pl.semaphore_signal(
-            barrier, inc=1, device_id={"dp": lax.rem(me + step, n_dp)}, device_id_type=MESH
-        )
-    pl.semaphore_wait(barrier, n_dp + n_t - 2)
+    peers = [{"tensor": lax.rem(rank + step, n_t)} for step in range(1, n_t)]
+    if all_dp:
+        peers += [{"dp": lax.rem(me + step, n_dp)} for step in range(1, n_dp)]
+    else:
+        peers += [{"dp": lax.rem(me + 2 * step, n_dp)} for step in range(1, n_dp // 2)]
+        peers += [{"dp": flip(me)}]
+    for peer in peers:
+        pl.semaphore_signal(barrier, inc=1, device_id=peer, device_id_type=MESH)
+    pl.semaphore_wait(barrier, len(peers))
 
 
 def send(src, dst, send_sem, recv_sem, device):
@@ -95,167 +93,140 @@
     return copy
 
 
-class DpGather:
-    def __init__(self, n_dp, me, own, full, sems):
-        self.n_outer = n_dp // 2
-        self.full, self.sems = full, sems
-        self.outer, self.inner = lax.div(me, 2), lax.rem(me, 2)
-        self.partner = {"dp": me + 1 - 2 * self.inner}
-        full[me] = own[...]
-        self.first, self.second = [], []
+class Gather:
+    def __init__(self, axis, count, me, full, sems):
+        self.axis, self.count, self.me, self.full, self.sems = axis, count, me, full, sems
+        self.n_outer = count // 2
+        self.first, self.second = {}, {}
         for step in range(1, self.n_outer):
-            peer = lax.rem(self.outer + step, self.n_outer) * 2 + self.inner
-            self.first.append(
-                send(full.at[me], full.at[me], sems.at[0, step], sems.at[1, step], {"dp": peer})
+            peer = {axis: lax.rem(me + 2 * step, count)}
+            self.first[step] = send(
+                full.at[me], full.at[me], sems.at[0, step], sems.at[1, step], peer
             )
-        self.second.append(
-            send(full.at[me], full.at[me], sems.at[2, 0], sems.at[3, 0], self.partner)
+        self.hand_on(0, me)
+
+    def hand_on(self, step, block):
+        self.second[step] = send(
+            self.full.at[block],
+            self.full.at[block],
+            self.sems.at[2, step],
+            self.sems.at[3, step],
+            {self.axis: flip(self.me)},
         )
 
-    def forward(self):
-        for step in range(1, self.n_outer):
-            self.first[step - 1].wait_recv()
-            source = lax.rem(self.outer + self.n_outer - step, self.n_outer) * 2 + self.inner
-            self.second.append(
-                send(
-                    self.full.at[source],
-                    self.full.at[source],
-                    self.sems.at[2, step],
-                    self.sems.at[3, step],
-                    self.partner,
-                )
-            )
+    def forward(self, step):
+        self.first[step].wait_recv()
+        self.hand_on(step, lax.rem(self.me + self.count - 2 * step, self.count))
 
     def finish(self):
-        for copy in self.second:
+        for copy in self.second.values():
             copy.wait_recv()
-        for copy in self.first + self.second:
+        for copy in list(self.first.values()) + list(self.second.values()):
             copy.wait_send()
 
 
-class DpReduce:
-    def __init__(self, n_dp, me, parts, pair, sums, far, sems):
-        self.n_outer = n_dp // 2
-        self.me, self.parts, self.pair, self.sums, self.far, self.sems = (
-            me, parts, pair, sums, far, sems,
-        )
-        self.outer, self.inner = lax.div(me, 2), lax.rem(me, 2)
-        partner = {"dp": me + 1 - 2 * self.inner}
+class Reduce:
+    def __init__(self, axis, count, me, parts, pair, sums, far, sems):
+        self.axis, self.count, self.me, self.parts = axis, count, me, parts
+        self.pair, self.sums, self.far, self.sems = pair, sums, far, sems
+        self.n_outer = count // 2
         self.first, self.second = {}, {}
         for step in list(range(1, self.n_outer)) + [0]:
-            block = lax.rem(self.outer + step, self.n_outer) * 2 + 1 - self.inner
+            block = lax.rem(flip(me) + 2 * step, count)
             self.first[step] = send(
-                parts.at[block], pair.at[step], sems.at[0, step], sems.at[1, step], partner
+                parts.at[block], pair.at[step], sems.at[0, step], sems.at[1, step],
+                {axis: flip(me)},
             )
 
-    def forward(self):
-        for step in range(1, self.n_outer):
-            self.first[step].wait_recv()
-            peer = lax.rem(self.outer + step, self.n_outer) * 2 + self.inner
-            self.sums[step] = (
-                self.parts[peer].astype(jnp.float32) + self.pair[step].astype(jnp.float32)
-            ).astype(jnp.bfloat16)
-            self.second[step] = send(
-                self.sums.at[step],
-                self.far.at[step],
-                self.sems.at[2, step],
-                self.sems.at[3, step],
-                {"dp": peer},
-            )
-
-    def finish(self, out):
+    def forward(self, step):
+        self.first[step].wait_recv()
+        peer = lax.rem(self.me + 2 * step, self.count)
+        self.sums[step] = (
+            self.parts[peer].astype(jnp.float32) + self.pair[step].astype(jnp.float32)
+        ).astype(jnp.bfloat16)
+        self.second[step] = send(
+            self.sums.at[step],
+            self.far.at[step],
+            self.sems.at[2, step],
+            self.sems.at[3, step],
+            {self.axis: peer},
+        )
+
+    def total(self):
         self.first[0].wait_recv()
         total = self.parts[self.me].astype(jnp.float32) + self.pair[0].astype(jnp.float32)
         for step in range(1, self.n_outer):
             self.second[step].wait_recv()
             total = total + self.far[step].astype(jnp.float32)
-        out[...] = total
+        return total
+
+    def finish(self):
         for copy in list(self.first.values()) + list(self.second.values()):
             copy.wait_send()
 
 
-def start_rows_sum(n_t, rank, parts, slots, sems):
-    copies = []
-    for step in range(1, n_t):
-        peer = lax.rem(rank + step, n_t)
-        copies.append(
-            send(parts.at[peer], slots.at[step - 1], sems.at[0, step], sems.at[1, step],
-                 {"tensor": peer})
-        )
-    return copies
-
-
-def end_rows_sum(n_t, rank, parts, slots, copies):
-    total = parts[rank].astype(jnp.float32)
-    for step in range(1, n_t):
-        copies[step - 1].wait_recv()
-        total = total + slots[step - 1].astype(jnp.float32)
-    return total
-
-
-def start_rows_gather(n_t, rank, full, sems):
-    return [
-        send(full.at[rank], full.at[rank], sems.at[0, step], sems.at[1, step],
-             {"tensor": lax.rem(rank + step, n_t)})
-        for step in range(1, n_t)
-    ]
-
-
-def end_sends(copies):
-    for copy in copies:
-        copy.wait_send()
-
-
-def end_all(copies):
-    for copy in copies:
-        copy.wait_recv()
-    end_sends(copies)
+def forward_all(stages, first=1):
+    last = max(stage.n_outer for stage in stages)
+    for step in range(first, last):
+        for stage in stages:
+            if step not in stage.second and step < stage.n_outer:
+                stage.forward(step)
 
 
 def gather_kernel(n_dp, n_t, w_ref, x_ref, cot_ref, w_all, x_all, cot_all, w_sems, x_sems, cot_sems):
-    me, rank = places(n_dp, n_t)
+    me, rank = lax.axis_index("dp"), lax.axis_index("tensor")
+    w_all[me] = w_ref[...]
     x_all[rank] = x_ref[...]
     cot_all[rank] = cot_ref[...]
     greet(n_dp, n_t, me, rank)
-    weights = DpGather(n_dp, me, w_ref, w_all, w_sems)
-    x_copies = start_rows_gather(n_t, rank, x_all, x_sems)
-    cot_copies = start_rows_gather(n_t, rank, cot_all, cot_sems)
-    weights.forward()
-    end_all(x_copies)
-    end_all(cot_copies)
+    weights = Gather("dp", n_dp, me, w_all, w_sems)
+    x_rows = Gather("tensor", n_t, rank, x_all, x_sems)
+    cot_rows = Gather("tensor", n_t, rank, cot_all, cot_sems)
+    forward_all([weights, x_rows])
+    forward_all([cot_rows])
+    x_rows.finish()
+    cot_rows.finish()
     weights.finish()
 
 
 def middle_kernel(
     n_dp, n_t, w_ref, part_ref, x_ref, gain_ref, w_all, residual_ref, mlp_all,
-    slots, w_sems, part_sems, row_sems,
+    pair, sums, far, w_sems, part_sems, row_sems,
 ):
-    me, rank = places(n_dp, n_t)
+    me, rank = lax.axis_index("dp"), lax.axis_index("tensor")
+    w_all[me] = w_ref[...]
     greet(n_dp, n_t, me, rank)
-    part_copies = start_rows_sum(n_t, rank, part_ref, slots, part_sems)
-    weights = DpGather(n_dp, me, w_ref, w_all, w_sems)
-    total = end_rows_sum(n_t, rank, part_ref, slots, part_copies)
-    residual = x_ref[...].astype(jnp.float32) + total
+    parts = Reduce("tensor", n_t, rank, part_ref, pair, sums, far, part_sems)
+    weights = Gather("dp", n_dp, me, w_all, w_sems)
+    forward_all([parts])
+    weights.forward(1)
+    residual = x_ref[...].astype(jnp.float32) + parts.total()
     residual_ref[...] = residual
     unit, unused_inverse = unit_rows(residual)
     mlp_all[rank] = (unit * gain_ref[...]).astype(jnp.bfloat16)
-    row_copies = start_rows_gather(n_t, rank, mlp_all, row_sems)
-    weights.forward()
-    end_all(row_copies)
-    end_sends(part_copies)
+    rows = Gather("tensor", n_t, rank, mlp_all, row_sems)
+    weights.forward(2)
+    forward_all([rows])
+    forward_all([weights])
+    rows.finish()
+    parts.finish()
     weights.finish()
 
 
 def turn_kernel(
     n_dp, n_t, grads_ref, back_ref, out_part_ref, residual_ref, gain_ref, cot_ref, valid_ref,
     w_sum, output_ref, grad_residual_ref, grad_all, gain_part,
-    back_slots, out_slots, pair, sums, far, back_sems, out_sems, w_sems, row_sems,
+    back_pair, back_sums, back_far, out_pair, out_sums, out_far, pair, sums, far,
+    back_sems, out_sems, w_sems, row_sems,
 ):
-    me, rank = places(n_dp, n_t)
+    me, rank = lax.axis_index("dp"), lax.axis_index("tensor")
     greet(n_dp, n_t, me, rank)
-    back_copies = start_rows_sum(n_t, rank, back_ref, back_slots, back_sems)
-    weights = DpReduce(n_dp, me, grads_ref, pair, sums, far, w_sems)
-    grad = end_rows_sum(n_t, rank, back_ref, back_slots, back_copies)
+    back = Reduce("tensor", n_t, rank, back_ref, back_pair, back_sums, back_far, back_sems)
+    weights = Reduce("dp", n_dp, me, grads_ref, pair, sums, far, w_sems)
+    forward_all([back])
+    mlp_out = Reduce("tensor", n_t, rank, out_part_ref, out_pair, out_sums, out_far, out_sems)
+    weights.forward(1)
+    grad = back.total()
     residual = residual_ref[...]
     valid = valid_ref[...]
     unit, inverse = unit_rows(residual)
@@ -265,28 +236,32 @@
     )
     grad_residual_ref[...] = grad_residual
     grad_all[rank] = grad_residual.astype(jnp.bfloat16)
-    row_copies = start_rows_gather(n_t, rank, grad_all, row_sems)
-    out_copies = start_rows_sum(n_t, rank, out_part_ref, out_slots, out_sems)
-    weights.forward()
-    end_all(row_copies)
-    mlp_out = end_rows_sum(n_t, rank, out_part_ref, out_slots, out_copies)
-    output_ref[...] = (valid * (residual + mlp_out)).astype(jnp.bfloat16)
-    end_sends(back_copies)
-    end_sends(out_copies)
-    weights.finish(w_sum)
+    rows = Gather("tensor", n_t, rank, grad_all, row_sems)
+    weights.forward(2)
+    forward_all([mlp_out])
+    forward_all([rows])
+    forward_all([weights])
+    output_ref[...] = (valid * (residual + mlp_out.total())).astype(jnp.bfloat16)
+    rows.finish()
+    back.finish()
+    mlp_out.finish()
+    w_sum[...] = weights.total()
+    weights.finish()
 
 
 def last_kernel(
     n_dp, n_t, grads_ref, back_ref, x_ref, gain_ref, grad_residual_ref, gain_part_ref,
     w_sum, input_grad_ref, gain_sum_ref,
-    back_slots, pair, sums, far, own_gain, near_gain, group_gain, far_gain,
+    back_pair, back_sums, back_far, pair, sums, far, own_gain, near_gain, group_gain, far_gain,
     back_sems, w_sems, near_sems, far_sems,
 ):
-    me, rank = places(n_dp, n_t)
-    greet(n_dp, n_t, me, rank)
-    back_copies = start_rows_sum(n_t, rank, back_ref, back_slots, back_sems)
-    weights = DpReduce(n_dp, me, grads_ref, pair, sums, far, w_sems)
-    grad = end_rows_sum(n_t, rank, back_ref, back_slots, back_copies)
+    me, rank = lax.axis_index("dp"), lax.axis_index("tensor")
+    greet(n_dp, n_t, me, rank, all_dp=True)
+    back = Reduce("tensor", n_t, rank, back_ref, back_pair, back_sums, back_far, back_sems)
+    weights = Reduce("dp", n_dp, me, grads_ref, pair, sums, far, w_sems)
+    forward_all([back])
+    weights.forward(1)
+    grad = back.total()
     unit, inverse = unit_rows(x_ref[...].astype(jnp.float32))
     width = unit.shape[1]
     own_gain[0:1, :] = jnp.sum(grad * unit, axis=0, keepdims=True)
@@ -297,6 +272,7 @@
              {"tensor": lax.rem(rank + step, n_t)})
         for step in range(1, n_t)
     ]
+    weights.forward(2)
     input_grad_ref[...] = (
         grad_residual_ref[...] + norm_back(unit, inverse, gain_ref[...], grad)
     ).astype(jnp.bfloat16)
@@ -310,15 +286,16 @@
              {"dp": lax.rem(me + step, n_dp)})
         for step in range(1, n_dp)
     ]
-    weights.forward()
+    forward_all([weights])
     for step in range(1, n_dp):
         far_copies[step - 1].wait_recv()
         total = total + far_gain[step - 1]
     gain_sum_ref[...] = total
-    end_sends(near)
-    end_sends(far_copies)
-    end_sends(back_copies)
-    weights.finish(w_sum)
+    for copy in near + far_copies:
+        copy.wait_send()
+    back.finish()
+    w_sum[...] = weights.total()
+    weights.finish()
 
 
 def call(kernel, n_dp, n_t, number, outs, scratch, operands):
@@ -359,7 +336,7 @@
         return pltpu.SemaphoreType.DMA(count)
 
     def row_sems():
-        return dma((2, n_t))
+        return dma((4, n_t // 2))
 
     segment, position = layout(seq_lengths[0], group_rows)
     valid_all = (segment < SEQS).astype(jnp.float32)[:, None]
@@ -413,7 +390,7 @@
     attn_part = dot(context, full_wo, ((1,), (1,))).astype(low)
 
     row_block = (n_t, local_rows, width)
-    slots = pltpu.VMEM((n_t - 1, local_rows, width), low)
+    slots = [pltpu.VMEM((n_t // 2, local_rows, width), low)] * 3
     second_all, residual, mlp_all = call(
         middle_kernel, n_dp, n_t, 2,
         [
@@ -421,7 +398,7 @@
             ((local_rows, width), jnp.float32),
             (row_block, low),
         ],
-        [slots, dma((4, n_outer)), row_sems(), row_sems()],
+        slots + [dma((4, n_outer)), row_sems(), row_sems()],
         (second_block, attn_part.reshape(row_block), inputs, gain_two),
     )
     full_wi = second_all[:, :, : 2 * hidden_cols].reshape(width, 2 * hidden_cols)
@@ -459,7 +436,7 @@
             (row_block, low),
             ((1, width), jnp.float32),
         ],
-        [slots, slots] + reduce_scratch(second_cols)
+        slots + slots + reduce_scratch(second_cols)
         + [row_sems(), row_sems(), dma((4, n_outer)), row_sems()],
         (
             second_grads, back_part.reshape(row_block), out_part.reshape(row_block),
@@ -511,13 +488,13 @@
             ((local_rows, width), low),
             ((8, width), jnp.float32),
         ],
-        [slots] + reduce_scratch(first_cols)
+        slots + reduce_scratch(first_cols)
         + [
             gain_block_f32,
             pltpu.VMEM((n_t - 1, 8, width), jnp.float32),
             gain_block_f32,
             pltpu.VMEM((n_dp - 1, 8, width), jnp.float32),
-            row_sems(), dma((4, n_outer)), row_sems(), dma((2, n_dp)),
+            row_sems(), dma((4, n_outer)), dma((2, n_t)), dma((2, n_dp)),
         ],
         (
             first_grads, attn_back.reshape(row_block), inputs, gain_one, grad_residual, gain_part,

time: 172 us -> 160 us (0.930)
  Pallas kernels: 115 us -> 103 us
    pallas_call x4, Pallas kernels: 115 us -> 103 us  [call(): pl.pallas_call(functools.partial(kernel, n_dp, n_t), out_shape=[jax.Shape...]
where the time goes in v2:
time: 160 us; the launch traced here: 159 us
  Pallas kernels  103 us (64%)
  local copies, waits for them, and re-layouts  22.3 us (14%)
  matrix products  19.8 us (12%)
  other arithmetic  12.7 us (8%)
    pallas_call x4, Pallas kernels, call(): pl.pallas_call(functools.partial(kernel, n_dp, n_t), out_shape=[jax.Shape...  103 us
    unnamed x62, local copies, waits for them, and re-layouts  10.9 us
    dot_general x12, matrix products, dot(): lax.dot_general(first, second, (dims, ((), ())), preferred_element_type=j...  9.33 us

profile of v2, /device:TPU:11, one launch (start us, length us, event | category | flops | bytes accessed | tf_op | source)
XLA Modules:
  0.0 159.1 jit_solution(10766320738005322687)
XLA Ops:
  0.7 0.9 broadcast_in_dim.24
  4.5 0.9 copy.49
  6.2 1.0 copy.47
  7.1 1.1 reshape.344
  8.3 1.1 copy.48
  9.6 1.0 fusion.31
  10.6 0.9 broadcast_compare_fusion
  11.5 23.0 %shard_map.152 = (bf16[8,112,768]{2,1,0:T(8,128)(2,1)S(1)}, bf16[4,128,768]{2,1,0:T(8,128)(2,1)S(1)}, bf16[4,128,768]{2,1,0:T(8,128)(2,1)S(1)}) custom-call(bf16[112,768]{1,0:T(8,128)(2,1)S(1)} %fusion.26.w_ref, bf16[128,768]{1,0:T(8,128)(2,1)S(1)} %copy-done, bf16[128,768]{1,0:T(8,128)(2,1)S(1)} %copy-done.1), custom_call_target="tpu_custom_call" | custom-call | bytes 1130496 | tf_op jit(solution)/shard_map/pallas_call | solution.py:304
  34.9 1.0 slice.112
  35.8 1.1 slice.102
  36.9 1.1 fusion.7
  38.0 1.1 convert_reduce_fusion
  39.5 1.2 fusion.6
  41.4 1.8 %fusion.46 = f32[512,3,3,64]{0,3,2,1:T(8,128)S(1)} fusion(bf16[512,768,1,1]{1,0,3,2:T(8,128)(2,1)} %bitcast.118, bf16[3,3,64,768]{3,2,1,0:T(8,128)(2,1)S(1)} %bitcast.115), kind=kOutput, calls=%fused_computation.111 | convolution fusion | flops 452984832 | bytes 2850816 | tf_op jit(solution)/shard_map/dot_general | solution.py:318
  43.5 0.8 copy-done.26
  44.4 2.9 %fusion.45 = (f32[3,512]{1,0:T(4,128)S(1)}, f32[3,512,512]{1,2,0:T(8,128)}) fusion(pred[512,512]{0,1:T(8,128)(4,1)S(1)} %copy-done.26, bf16[512,3,32]{0,2,1:T(8,128)(2,1)S(1)} %get-tuple-element.89, bf16[512,3,32]{0,2,1:T(8,128)(2,1)S(1)} %get-tuple-element.90, bf16[512,3,32]{0,2,1:T(8,128)(2,1)S(1)} %get-tuple-element.84, ...), kind=kOutput, calls=%fused_computation.110 | convolution fusion | flops 104595968 | bytes 3807232 | tf_op jit(solution)/shard_map/sub | solution.py:382
  47.3 2.4 %convolution_convert_fusion.10 = bf16[3,64,512]{2,1,0:T(8,128)(2,1)S(1)} fusion(f32[512,3,3,64]{0,3,2,1:T(8,128)S(1)} %fusion.46, f32[3,512,512]{1,2,0:T(8,128)} %get-tuple-element.99, f32[3,512]{1,0:T(4,128)S(1)} %get-tuple-element.98), kind=kOutput, calls=%fused_computation.36 | convolution fusion | flops 102334464 | bytes 3547136 | tf_op jit(solution)/shard_map/hqk,khd->qhd/dot_general | solution.py:386
  50.1 24.0 %shard_map.153 = (bf16[8,96,864]{2,1,0:T(8,128)(2,1)S(1)}, f32[128,768]{1,0:T(8,128)S(1)}, bf16[4,128,768]{2,1,0:T(8,128)(2,1)S(1)}) custom-call(bf16[96,864]{1,0:T(8,128)(2,1)S(1)} %pad_maximum_fusion.8.w_ref, bf16[4,128,768]{2,1,0:T(8,128)(2,1)S(1)} %bitcast.105, bf16[128,768]{1,0:T(8,128)(2,1)S(1)} %copy-done, f32[1,768]{1,0:T(1,128)S(1)} %reshape.365.gain_ref), custom_call_target="tpu_custom_call" | custom-call | bytes 2304000 | tf_op jit(solution)/shard_map/pallas_call | solution.py:304
  77.5 0.8 convolution_convert_fusion.3
  79.0 1.2 pad_maximum_fusion
  80.1 2.0 %copy.53 = bf16[768,864]{1,0:T(8,128)(2,1)S(1)} copy(bf16[768,864]{0,1:T(8,128)(2,1)} %pad_maximum_fusion) | data formatting | bytes 2654208 | tf_op jit(solution)/shard_map/concatenate | solution.py:419
  82.1 1.7 %convolution_convert_fusion.5 = bf16[512,768]{1,0:T(8,128)(2,1)S(1)} fusion(bf16[512,288]{0,1:T(8,128)(2,1)S(1)} %get-tuple-element.76, bf16[768,288]{1,0:T(8,128)(2,1)} %bitcast.121), kind=kOutput, calls=%fused_computation.25 | convolution fusion | flops 226885632 | bytes 1523712 | tf_op jit(solution)/shard_map/dot_general | solution.py:318
  83.9 28.8 %shard_map.154 = (f32[96,864]{1,0:T(8,128)S(1)}, bf16[128,768]{1,0:T(8,128)(2,1)S(1)}, f32[128,768]{1,0:T(8,128)S(1)}, bf16[4,128,768]{2,1,0:T(8,128)(2,1)S(1)}, f32[1,768]{1,0:T(1,128)S(1)}) custom-call(bf16[8,96,864]{2,1,0:T(8,128)(2,1)S(1)} %bitcast.101, bf16[4,128,768]{2,1,0:T(8,128)(2,1)S(1)} %bitcast.110, bf16[4,128,768]{2,1,0:T(8,128)(2,1)S(1)} %bitcast.106, ...), custom_call_target="tpu_custom_call" | custom-call | bytes 6986752 | tf_op jit(solution)/shard_map/pallas_call | solution.py:304
  114.3 0.9 reshape.363
  115.3 2.6 %fusion.13 = bf16[512,1,3,64]{0,3,2,1:T(8,128)(2,1)S(1)} fusion(bf16[512,3,64]{0,2,1:T(8,128)(2,1)S(1)} %bitcast.131, f32[3,512,512]{1,2,0:T(8,128)} %get-tuple-element.99, f32[3,512]{1,0:T(4,128)S(1)} %get-tuple-element.98), kind=kOutput, calls=%fused_computation.37 | convolution fusion | flops 102334464 | bytes 3545088 | tf_op jit(solution)/shard_map/hqk,qhd->khd/dot_general | solution.py:449
  118.1 1.6 %multiply_reduce_fusion = (f32[3,512]{1,0:T(4,128)S(1)}, f32[3,512,512]{1,2,0:T(8,128)S(1)}) fusion(f32[3,512,512]{1,2,0:T(8,128)S(1)} %copy-done.12, f32[3,512]{1,0:T(4,128)S(1)} %get-tuple-element.98, bf16[512,3,64]{0,2,1:T(8,128)(2,1)S(1)} %bitcast.132, f32[512,3,3,64]{0,3,2,1:T(8,128)} %copy-done.9), kind=kOutput, calls=%fused_computation.2 | convolution fusion | flops 103021056 | bytes 6696960 | tf_op jit(solution)/shard_map/qhd,khd->hqk/dot_general | solution.py:452
  119.8 0.9 multiply_convert_fusion
  122.8 0.9 copy-done.6
  125.2 1.1 pad_maximum_fusion.1
  126.3 1.6 copy.58
  127.9 27.3 %shard_map.155 = (f32[96,768]{1,0:T(8,128)S(1)}, bf16[128,768]{1,0:T(8,128)(2,1)S(1)}, f32[8,768]{1,0:T(8,128)S(1)}) custom-call(bf16[8,96,768]{2,1,0:T(8,128)(2,1)S(1)} %bitcast.102, bf16[4,128,768]{2,1,0:T(8,128)(2,1)S(1)} %bitcast.109, bf16[128,768]{1,0:T(8,128)(2,1)S(1)} %copy-done, f32[1,768]{1,0:T(1,128)S(1)} %reshape.368.gain_ref, ...), custom_call_target="tpu_custom_call" | custom-call | bytes 5124096 | tf_op jit(solution)/shard_map/pallas_call | solution.py:304
  156.8 0.9 copy.60
  (107 shorter events, 18.3 us)
Async XLA Ops:
  0.6 10.9 %copy-start = (bf16[128,768]{1,0:T(8,128)(2,1)S(1)}, bf16[128,768]{1,0:T(8,128)(2,1)}, u32[]{:S(2)}) copy-start(bf16[128,768]{1,0:T(8,128)(2,1)} %x_ref.5) | copy-start | bytes 589828
  0.6 10.9 %copy-start.1 = (bf16[128,768]{1,0:T(8,128)(2,1)S(1)}, bf16[128,768]{1,0:T(8,128)(2,1)}, u32[]{:S(2)}) copy-start(bf16[128,768]{1,0:T(8,128)(2,1)} %cot_ref.3) | copy-start | bytes 589828
  39.1 1.6 %copy-start.5 = (bf16[8,96,576]{2,1,0:T(8,128)(2,1)S(1)}, bf16[8,96,576]{2,1,0:T(8,128)(2,1)}, u32[]{:S(2)}) copy-start(bf16[8,96,576]{2,1,0:T(8,128)(2,1)} %slice.102) | copy-start | bytes 2654212
  41.4 2.0 %copy-start.15 = (f32[512,32]{0,1:T(8,128)S(1)}, f32[512,32]{0,1:T(8,128)}, u32[]{:S(2)}) copy-start(f32[512,32]{0,1:T(8,128)} %get-tuple-element.93) | copy-start | bytes 196612
  41.4 2.0 %copy-start.25 = (f32[512,32]{0,1:T(8,128)S(1)}, f32[512,32]{0,1:T(8,128)}, u32[]{:S(2)}) copy-start(f32[512,32]{0,1:T(8,128)} %get-tuple-element.92) | copy-start | bytes 196612
  43.2 4.1 %copy-start.9 = (f32[512,3,3,64]{0,3,2,1:T(8,128)}, f32[512,3,3,64]{0,3,2,1:T(8,128)S(1)}, u32[]{:S(2)}) copy-start(f32[512,3,3,64]{0,3,2,1:T(8,128)S(1)} %fusion.46) | copy-start | bytes 3538948
  43.2 1.1 copy-start.26
  43.5 3.8 %copy-start.16 = (bf16[512,3,32]{0,2,1:T(8,128)(2,1)}, bf16[512,3,32]{0,2,1:T(8,128)(2,1)S(1)}, u32[]{:S(2)}) copy-start(bf16[512,3,32]{0,2,1:T(8,128)(2,1)S(1)} %get-tuple-element.89) | copy-start | bytes 294916
  43.5 3.8 %copy-start.18 = (bf16[512,3,32]{0,2,1:T(8,128)(2,1)}, bf16[512,3,32]{0,2,1:T(8,128)(2,1)S(1)}, u32[]{:S(2)}) copy-start(bf16[512,3,32]{0,2,1:T(8,128)(2,1)S(1)} %get-tuple-element.90) | copy-start | bytes 294916
  43.5 3.8 %copy-start.20 = (bf16[512,3,32]{0,2,1:T(8,128)(2,1)}, bf16[512,3,32]{0,2,1:T(8,128)(2,1)S(1)}, u32[]{:S(2)}) copy-start(bf16[512,3,32]{0,2,1:T(8,128)(2,1)S(1)} %get-tuple-element.83) | copy-start | bytes 294916
  43.5 3.8 %copy-start.22 = (bf16[512,3,32]{0,2,1:T(8,128)(2,1)}, bf16[512,3,32]{0,2,1:T(8,128)(2,1)S(1)}, u32[]{:S(2)}) copy-start(bf16[512,3,32]{0,2,1:T(8,128)(2,1)S(1)} %get-tuple-element.84) | copy-start | bytes 294916
  47.3 2.4 %copy-start.7 = (bf16[8,96,192]{2,1,0:T(8,128)(2,1)S(1)}, bf16[8,96,192]{2,1,0:T(8,128)(2,1)}, u32[]{:S(2)}) copy-start(bf16[8,96,192]{2,1,0:T(8,128)(2,1)} %slice.112) | copy-start | bytes 884740
  74.1 0.8 copy-start.2
  74.3 1.2 copy-start.13
  74.8 1.1 copy-start.14
  76.0 1.1 copy-start.10
  80.1 3.7 %copy-start.4 = (f32[128,1]{1,0:T(8,128)S(1)}, f32[128,1]{1,0:T(8,128)}, u32[]{:S(2)}) copy-start(f32[128,1]{1,0:T(8,128)} %copy.54.valid_ref) | copy-start | bytes 1540
  82.1 1.7 %copy-start.3 = (f32[128,768]{1,0:T(8,128)S(1)}, f32[128,768]{1,0:T(8,128)}, u32[]{:S(2)}) copy-start(f32[128,768]{1,0:T(8,128)} %copy-done.2) | copy-start | bytes 1179652
  83.9 28.8 %copy-start.8 = (bf16[8,96,192]{2,1,0:T(8,128)(2,1)S(1)}, bf16[8,96,192]{2,1,0:T(8,128)(2,1)}, u32[]{:S(2)}) copy-start(bf16[8,96,192]{2,1,0:T(8,128)(2,1)} %slice.112) | copy-start | bytes 884740
  115.3 2.8 %copy-start.12 = (f32[3,512,512]{1,2,0:T(8,128)S(1)}, f32[3,512,512]{1,2,0:T(8,128)}, u32[]{:S(2)}) copy-start(f32[3,512,512]{1,2,0:T(8,128)} %get-tuple-element.99) | copy-start | bytes 9437188
  119.8 0.9 copy-start.21
  119.8 0.9 copy-start.23
  120.7 0.9 copy-start.17
  120.7 0.9 copy-start.19
  121.7 0.8 copy-start.24
  122.5 1.2 copy-start.6
  122.8 1.8 %copy-start.11 = (bf16[4,128,768]{2,1,0:T(8,128)(2,1)S(1)}, bf16[4,128,768]{2,1,0:T(8,128)(2,1)}, u32[]{:S(2)}) copy-start(bf16[4,128,768]{2,1,0:T(8,128)(2,1)} %fusion.6) | copy-start | bytes 2359300

commit v3 on v2

--- a/solution.py
+++ b/solution.py
@@ -17,15 +17,22 @@
 
 
 def layout(lengths, row_count):
-    seq_ends = jnp.cumsum(lengths)
     row_ids = jnp.arange(row_count, dtype=jnp.int32)
-    segment = jnp.sum((row_ids[None, :] >= seq_ends[:, None]).astype(jnp.int32), axis=0)
-    starts = jnp.concatenate([seq_ends - lengths, seq_ends[-1:]])
-    slot_ids = jnp.arange(lengths.shape[0] + 1, dtype=jnp.int32)
-    seq_begin = jnp.sum(
-        jnp.where(segment[None, :] == slot_ids[:, None], starts[:, None], 0), axis=0
-    )
-    return (segment, row_ids - seq_begin)
+    segment, begin, end = jnp.zeros_like(row_ids), jnp.zeros_like(row_ids), 0
+    for slot in range(SEQS):
+        end = end + lengths[slot]
+        past = row_ids >= end
+        segment = segment + past.astype(jnp.int32)
+        begin = begin + jnp.where(past, lengths[slot], 0)
+    return (segment, row_ids - begin)
+
+
+def valid_mask(lengths_ref, first_row, row_count):
+    used = lengths_ref[0, 0]
+    for slot in range(1, SEQS):
+        used = used + lengths_ref[0, slot]
+    row_ids = lax.broadcasted_iota(jnp.int32, (row_count, 1), 0) + first_row
+    return (row_ids < used).astype(jnp.float32)
 
 
 def unit_rows(array_in):
@@ -118,25 +125,42 @@
         self.first[step].wait_recv()
         self.hand_on(step, lax.rem(self.me + self.count - 2 * step, self.count))
 
-    def finish(self):
+    def arrive(self):
         for copy in self.second.values():
             copy.wait_recv()
+
+    def leave(self):
         for copy in list(self.first.values()) + list(self.second.values()):
             copy.wait_send()
 
+    def finish(self):
+        self.arrive()
+        self.leave()
+
 
 class Reduce:
-    def __init__(self, axis, count, me, parts, pair, sums, far, sems):
+    def __init__(self, axis, count, me, parts, pair, sums, far, sems, pieces=()):
         self.axis, self.count, self.me, self.parts = axis, count, me, parts
+        self.pieces = pieces
         self.pair, self.sums, self.far, self.sems = pair, sums, far, sems
         self.n_outer = count // 2
         self.first, self.second = {}, {}
         for step in list(range(1, self.n_outer)) + [0]:
             block = lax.rem(flip(me) + 2 * step, count)
+            self.pack(block)
             self.first[step] = send(
                 parts.at[block], pair.at[step], sems.at[0, step], sems.at[1, step],
                 {axis: flip(me)},
             )
+        for step in range(self.n_outer):
+            self.pack(lax.rem(me + 2 * step, count))
+
+    def pack(self, block):
+        column = 0
+        for piece in self.pieces:
+            width = piece.shape[2]
+            self.parts[block, :, column : column + width] = piece[block]
+            column += width
 
     def forward(self, step):
         self.first[step].wait_recv()
@@ -173,7 +197,11 @@
                 stage.forward(step)
 
 
-def gather_kernel(n_dp, n_t, w_ref, x_ref, cot_ref, w_all, x_all, cot_all, w_sems, x_sems, cot_sems):
+def gather_kernel(
+    n_dp, n_t, lengths_ref, w_ref, x_ref, cot_ref,
+    qkv_all, wo_all, attn_all, grad_all, gain_one, gain_two,
+    w_all, x_all, cot_all, units, w_sems, x_sems, cot_sems,
+):
     me, rank = lax.axis_index("dp"), lax.axis_index("tensor")
     w_all[me] = w_ref[...]
     x_all[rank] = x_ref[...]
@@ -182,11 +210,29 @@
     weights = Gather("dp", n_dp, me, w_all, w_sems)
     x_rows = Gather("tensor", n_t, rank, x_all, x_sems)
     cot_rows = Gather("tensor", n_t, rank, cot_all, cot_sems)
-    forward_all([weights, x_rows])
-    forward_all([cot_rows])
-    x_rows.finish()
-    cot_rows.finish()
-    weights.finish()
+    weights.forward(1)
+    forward_all([x_rows, cot_rows])
+    forward_all([weights])
+    x_rows.arrive()
+    cot_rows.arrive()
+    row_count, width = x_ref.shape
+    for block in range(n_t):
+        unit, unused_inverse = unit_rows(x_all[block].astype(jnp.float32))
+        units[block] = unit
+        valid = valid_mask(lengths_ref, block * row_count, row_count)
+        grad_all[block] = (valid * cot_all[block].astype(jnp.float32)).astype(jnp.bfloat16)
+    weights.arrive()
+    gains = jnp.sum(w_all[:, :GAIN_ROWS, :width].astype(jnp.float32), axis=0)
+    gain_one[...] = gains[0:1]
+    gain_two[...] = gains[1:2]
+    for block in range(n_t):
+        attn_all[block] = (units[block] * gains[0:1]).astype(jnp.bfloat16)
+    split = qkv_all.shape[2]
+    qkv_all[...] = w_all[:, GAIN_ROWS:, :split]
+    wo_all[...] = w_all[:, GAIN_ROWS:, split:]
+    x_rows.leave()
+    cot_rows.leave()
+    weights.leave()
 
 
 def middle_kernel(
@@ -214,21 +260,25 @@
 
 
 def turn_kernel(
-    n_dp, n_t, grads_ref, back_ref, out_part_ref, residual_ref, gain_ref, cot_ref, valid_ref,
+    n_dp, n_t, lengths_ref, piece_one, piece_two, back_ref, out_part_ref, residual_ref, gain_ref,
+    cot_ref,
     w_sum, output_ref, grad_residual_ref, grad_all, gain_part,
-    back_pair, back_sums, back_far, out_pair, out_sums, out_far, pair, sums, far,
+    back_pair, back_sums, back_far, out_pair, out_sums, out_far, grads, pair, sums, far,
     back_sems, out_sems, w_sems, row_sems,
 ):
     me, rank = lax.axis_index("dp"), lax.axis_index("tensor")
     greet(n_dp, n_t, me, rank)
     back = Reduce("tensor", n_t, rank, back_ref, back_pair, back_sums, back_far, back_sems)
-    weights = Reduce("dp", n_dp, me, grads_ref, pair, sums, far, w_sems)
+    weights = Reduce(
+        "dp", n_dp, me, grads, pair, sums, far, w_sems, (piece_one, piece_two)
+    )
     forward_all([back])
     mlp_out = Reduce("tensor", n_t, rank, out_part_ref, out_pair, out_sums, out_far, out_sems)
     weights.forward(1)
     grad = back.total()
     residual = residual_ref[...]
-    valid = valid_ref[...]
+    row_count = residual.shape[0]
+    valid = valid_mask(lengths_ref, rank * row_count, row_count)
     unit, inverse = unit_rows(residual)
     gain_part[...] = jnp.sum(grad * unit, axis=0, keepdims=True)
     grad_residual = valid * cot_ref[...].astype(jnp.float32) + norm_back(
@@ -250,15 +300,17 @@
 
 
 def last_kernel(
-    n_dp, n_t, grads_ref, back_ref, x_ref, gain_ref, grad_residual_ref, gain_part_ref,
+    n_dp, n_t, piece_one, piece_two, back_ref, x_ref, gain_ref, grad_residual_ref, gain_part_ref,
     w_sum, input_grad_ref, gain_sum_ref,
-    back_pair, back_sums, back_far, pair, sums, far, own_gain, near_gain, group_gain, far_gain,
+    back_pair, back_sums, back_far, grads, pair, sums, far, own_gain, near_gain, group_gain, far_gain,
     back_sems, w_sems, near_sems, far_sems,
 ):
     me, rank = lax.axis_index("dp"), lax.axis_index("tensor")
     greet(n_dp, n_t, me, rank, all_dp=True)
     back = Reduce("tensor", n_t, rank, back_ref, back_pair, back_sums, back_far, back_sems)
-    weights = Reduce("dp", n_dp, me, grads_ref, pair, sums, far, w_sems)
+    weights = Reduce(
+        "dp", n_dp, me, grads, pair, sums, far, w_sems, (piece_one, piece_two)
+    )
     forward_all([back])
     weights.forward(1)
     grad = back.total()
@@ -304,7 +356,10 @@
     return pl.pallas_call(
         functools.partial(kernel, n_dp, n_t),
         out_shape=[jax.ShapeDtypeStruct(shape, kind) for shape, kind in outs],
-        in_specs=[in_vmem] * len(operands),
+        in_specs=[
+            pl.BlockSpec(memory_space=pltpu.SMEM) if op.dtype == jnp.int32 else in_vmem
+            for op in operands
+        ],
         out_specs=[in_vmem] * len(outs),
         scratch_shapes=scratch,
         compiler_params=pltpu.CompilerParams(
@@ -339,37 +394,40 @@
         return dma((4, n_t // 2))
 
     segment, position = layout(seq_lengths[0], group_rows)
-    valid_all = (segment < SEQS).astype(jnp.float32)[:, None]
-    valid_rows = lax.dynamic_slice_in_dim(valid_all, rank * local_rows, local_rows)
     cosine, sine_table = rotation(position)
 
-    gain_row = jnp.concatenate([attn_gain, mlp_gain])
-    gain_block = jnp.zeros((GAIN_ROWS, first_cols), low).at[0, : 2 * depth].set(gain_row)
+    gain_block = lax.dynamic_update_slice(
+        jnp.zeros((GAIN_ROWS, first_cols), low), jnp.stack([attn_gain, mlp_gain]), (0, me * depth)
+    )
     first_block = jnp.concatenate(
-        [jnp.concatenate([wqkv.reshape(depth, 3 * head_cols), wo.T], axis=1), gain_block], axis=0
+        [gain_block, jnp.concatenate([wqkv.reshape(depth, 3 * head_cols), wo.T], axis=1)], axis=0
     )
     second_block = jnp.concatenate([wi.reshape(depth, 2 * hidden_cols), wo2.T], axis=1)
 
-    first_all, x_all, cot_all = call(
+    row_block = (n_t, local_rows, width)
+    full_qkv, full_wo, attn_all, grad_mlp_all, gain_one, gain_two = call(
         gather_kernel, n_dp, n_t, 1,
         [
-            ((n_dp,) + first_block.shape, low),
-            ((n_t, local_rows, width), low),
-            ((n_t, local_rows, width), low),
-        ],
-        [dma((4, n_outer)), row_sems(), row_sems()],
-        (first_block, inputs, cotangent),
-    )
-    full_qkv = first_all[:, :depth, : 3 * head_cols].reshape(width, 3 * head_cols)
-    full_wo = first_all[:, :depth, 3 * head_cols :].reshape(width, wo.shape[0])
-    gain_one = first_all[:, depth, :depth].reshape(1, width).astype(jnp.float32)
-    gain_two = first_all[:, depth, depth : 2 * depth].reshape(1, width).astype(jnp.float32)
-    grad_mlp_all = (
-        valid_all * cot_all.reshape(group_rows, width).astype(jnp.float32)
-    ).astype(low)
-
-    unit, unused_inverse = unit_rows(x_all.reshape(group_rows, width).astype(jnp.float32))
-    attn_all = (unit * gain_one).astype(low)
+            ((n_dp, depth, 3 * head_cols), low),
+            ((n_dp, depth, wo.shape[0]), low),
+            (row_block, low),
+            (row_block, low),
+            ((1, width), jnp.float32),
+            ((1, width), jnp.float32),
+        ],
+        [
+            pltpu.VMEM((n_dp,) + first_block.shape, low),
+            pltpu.VMEM(row_block, low),
+            pltpu.VMEM(row_block, low),
+            pltpu.VMEM(row_block, jnp.float32),
+            dma((4, n_outer)), row_sems(), row_sems(),
+        ],
+        (seq_lengths, first_block, inputs, cotangent),
+    )
+    full_qkv = full_qkv.reshape(width, 3 * head_cols)
+    full_wo = full_wo.reshape(width, wo.shape[0])
+    attn_all = attn_all.reshape(group_rows, width)
+    grad_mlp_all = grad_mlp_all.reshape(group_rows, width)
     qkv = dot(attn_all, full_qkv, ((1,), (0,))).reshape(group_rows, 3, heads_here, HEAD_DIM)
     query_low = rotate(qkv[:, 0], cosine, sine_table).astype(low)
     key_low = rotate(qkv[:, 1], cosine, sine_table).astype(low)
@@ -389,7 +447,6 @@
     )
     attn_part = dot(context, full_wo, ((1,), (1,))).astype(low)
 
-    row_block = (n_t, local_rows, width)
     slots = [pltpu.VMEM((n_t // 2, local_rows, width), low)] * 3
     second_all, residual, mlp_all = call(
         middle_kernel, n_dp, n_t, 2,
@@ -416,16 +473,13 @@
         [grad_hidden * other * slope, grad_hidden * gelu], axis=1
     ).astype(low)
     back_part = dot(grad_proj, full_wi, ((1,), (1,))).astype(low)
-    second_grads = jnp.concatenate(
-        [
-            dot(mlp_all, grad_proj, ((0,), (0,))).astype(low),
-            dot(grad_mlp_all, hidden, ((0,), (0,))).astype(low),
-        ],
-        axis=1,
-    ).reshape(n_dp, depth, second_cols)
+    wi_grad = dot(mlp_all, grad_proj, ((0,), (0,))).astype(low)
+    wo2_grad = dot(grad_mlp_all, hidden, ((0,), (0,))).astype(low)
 
     def reduce_scratch(cols):
-        return [pltpu.VMEM((n_outer, depth, cols), low)] * 3
+        return [pltpu.VMEM((n_dp, depth, cols), low)] + [
+            pltpu.VMEM((n_outer, depth, cols), low)
+        ] * 3
 
     second_sum, output, grad_residual, grad_all, gain_part = call(
         turn_kernel, n_dp, n_t, 3,
@@ -439,8 +493,11 @@
         slots + slots + reduce_scratch(second_cols)
         + [row_sems(), row_sems(), dma((4, n_outer)), row_sems()],
         (
-            second_grads, back_part.reshape(row_block), out_part.reshape(row_block),
-            residual, gain_two, cotangent, valid_rows,
+            seq_lengths,
+            wi_grad.reshape(n_dp, depth, 2 * hidden_cols),
+            wo2_grad.reshape(n_dp, depth, wo2.shape[0]),
+            back_part.reshape(row_block), out_part.reshape(row_block),
+            residual, gain_two, cotangent,
         ),
     )
     grad_all = grad_all.reshape(group_rows, width)
@@ -471,13 +528,8 @@
         axis=1,
     )
     grad_qkv = grad_qkv.astype(low).reshape(group_rows, 3 * head_cols)
-    first_grads = jnp.concatenate(
-        [
-            dot(attn_all, grad_qkv, ((0,), (0,))).astype(low),
-            dot(grad_all, context, ((0,), (0,))).astype(low),
-        ],
-        axis=1,
-    ).reshape(n_dp, depth, first_cols)
+    wqkv_grad = dot(attn_all, grad_qkv, ((0,), (0,))).astype(low)
+    wo_grad = dot(grad_all, context, ((0,), (0,))).astype(low)
     attn_back = dot(grad_qkv, full_qkv, ((1,), (1,))).astype(low)
 
     gain_block_f32 = pltpu.VMEM((8, width), jnp.float32)
@@ -497,7 +549,9 @@
             row_sems(), dma((4, n_outer)), dma((2, n_t)), dma((2, n_dp)),
         ],
         (
-            first_grads, attn_back.reshape(row_block), inputs, gain_one, grad_residual, gain_part,
+            wqkv_grad.reshape(n_dp, depth, 3 * head_cols),
+            wo_grad.reshape(n_dp, depth, wo.shape[0]),
+            attn_back.reshape(row_block), inputs, gain_one, grad_residual, gain_part,
         ),
     )
     gains_here = lax.dynamic_slice_in_dim(gain_sum[:2], me * depth, depth, axis=1)

time: 160 us -> 162 us (1.012)
  other arithmetic: 12.7 us -> 5.28 us
  matrix products: 19.8 us -> 25.7 us
  Pallas kernels: 103 us -> 105 us
    dot_general x12, matrix products: 9.33 us -> 14 us  [dot(): lax.dot_general(first, second, (dims, ((), ())), preferred_element_type=j...]
    convert_element_type x3 -> x4, local copies, waits for them, and re-layouts: 0.23 us -> 4.73 us  [the longest x1 1.71 us: shards(): wi_grad = dot(mlp_all, grad_proj, ((0,), (0,))).astype(low)]
    concatenate x5 -> x1, other arithmetic: 3.82 us -> 0.09 us  [shards(): jnp.concatenate([gain_block, jnp.concatenate([wqkv.reshape(depth, 3 * hea...]
    concatenate x2 -> x0, local copies, waits for them, and re-layouts: 3.56 us -> none  [the longest x1 1.99 us: shards(): jnp.concatenate([dot(mlp_all, grad_proj, ((0,), (0,))).astype(low), dot(g...]
    convert_element_type x5 -> x0, other arithmetic: 2.39 us -> none  [the longest x1 1.2 us: shards(): attn_all = (unit * gain_one).astype(low)]
    unnamed x62 -> x72, local copies, waits for them, and re-layouts: 10.9 us -> 8.7 us
    reduce_sum x4 -> x0, other arithmetic: 1.7 us -> none  [the longest x1 1.15 us: unit_rows(): row_mean = jnp.mean(array_in, axis=-1, keepdims=True)]
where the time goes in v3:
time: 162 us; the launch traced here: 160 us
  Pallas kernels  105 us (65%)
  matrix products  25.7 us (16%)
  local copies, waits for them, and re-layouts  22 us (14%)
  other arithmetic  5.28 us (3%)
  between operations  2.52 us (2%)
    pallas_call x4, Pallas kernels, call(): pl.pallas_call(functools.partial(kernel, n_dp, n_t), out_shape=[jax.Shape...  105 us
    dot_general x12, matrix products, dot(): lax.dot_general(first, second, (dims, ((), ())), preferred_element_type=j...  14 us
    unnamed x72, local copies, waits for them, and re-layouts  8.7 us
    sub x1, matrix products, shards(): exponent = jnp.exp(scores - jnp.max(scores, axis=-1, keepdims=True))  3.99 us

profile of v3, /device:TPU:11, one launch (start us, length us, event | category | flops | bytes accessed | tf_op | source)
XLA Modules:
  0.0 160.1 jit_solution(17330435823045519945)
XLA Ops:
  1.4 1.3 fusion.34
  4.0 1.3 subtract_convert_fusion.4
  5.9 0.9 copy.34
  6.8 1.0 copy.32
  7.8 1.1 reshape.236
  9.0 1.1 copy.33
  10.3 1.0 fusion.23
  11.3 0.9 broadcast_compare_fusion
  12.2 23.0 %shard_map.152 = (bf16[8,96,576]{2,1,0:T(8,128)(2,1)S(1)}, bf16[8,96,192]{2,1,0:T(8,128)(2,1)S(1)}, bf16[4,128,768]{2,1,0:T(8,128)(2,1)S(1)}, bf16[4,128,768]{2,...) custom-call(s32[1,2]{1,0:T(1,128)S(1)} %copy-done.11, bf16[112,768]{1,0:T(8,128)(2,1)S(1)} %maximum_maximum_fusion.w_ref, ...), custom_call_target="tpu_custom_call" | custom-call | bytes 1130512 | tf_op jit(solution)/shard_map/pallas_call | solution.py:356
  35.2 1.3 copy.36
  36.5 1.9 %fusion.36 = f32[512,3,3,64]{0,3,2,1:T(8,128)S(1)} fusion(bf16[512,768,1,1]{1,0,3,2:T(8,128)(2,1)S(1)} %bitcast.106, bf16[3,3,64,768]{3,2,1,0:T(8,128)(2,1)} %bitcast.114), kind=kOutput, calls=%fused_computation.87 | convolution fusion | flops 452984832 | bytes 2850816 | tf_op jit(solution)/shard_map/dot_general | solution.py:373
  38.5 1.0 copy-done.12
  39.6 4.0 %fusion.35 = (f32[3,512]{1,0:T(4,128)S(1)}, f32[3,512,512]{1,2,0:T(8,128)}) fusion(pred[512,512]{0,1:T(8,128)(4,1)} %broadcast_compare_fusion, bf16[512,3,32]{0,2,1:T(8,128)(2,1)S(1)} %get-tuple-element.73, bf16[512,3,32]{0,2,1:T(8,128)(2,1)S(1)} %get-tuple-element.74, bf16[512,3,32]{0,2,1:T(8,128)(2,1)S(1)} %get-tuple-element.68, ...), kind=kOutput, calls=%fused_computation.86 | convolution fusion | flops 104595968 | bytes 3807232 | tf_op jit(solution)/shard_map/sub | solution.py:440
  43.6 2.4 %convolution_convert_fusion.10 = bf16[3,64,512]{2,1,0:T(8,128)(2,1)S(1)} fusion(f32[512,3,3,64]{0,3,2,1:T(8,128)} %copy-done.12, f32[3,512,512]{1,2,0:T(8,128)} %get-tuple-element.83, f32[3,512]{1,0:T(4,128)S(1)} %get-tuple-element.82), kind=kOutput, calls=%fused_computation.24 | convolution fusion | flops 102334464 | bytes 3545088 | tf_op jit(solution)/shard_map/hqk,khd->qhd/dot_general | solution.py:444
  46.7 24.7 %shard_map.153 = (bf16[8,96,864]{2,1,0:T(8,128)(2,1)S(1)}, f32[128,768]{1,0:T(8,128)S(1)}, bf16[4,128,768]{2,1,0:T(8,128)(2,1)S(1)}) custom-call(bf16[96,864]{1,0:T(8,128)(2,1)S(1)} %pad_maximum_fusion.6.w_ref, bf16[4,128,768]{2,1,0:T(8,128)(2,1)S(1)} %bitcast.97, bf16[128,768]{1,0:T(8,128)(2,1)S(1)} %copy-done, f32[1,768]{1,0:T(1,128)S(1)} %get-tuple-element.28.gain_ref), custom_call_target="tpu_custom_call" | custom-call | bytes 2304000 | tf_op jit(solution)/shard_map/pallas_call | solution.py:356
  73.2 1.2 convolution_convert_fusion.6
  74.4 1.8 %convolution_convert_fusion.3 = bf16[512,768]{1,0:T(8,128)(2,1)} fusion(bf16[768,576]{1,0:T(8,128)(2,1)S(1)} %bitcast.113, bf16[512,288]{0,1:T(8,128)(2,1)S(1)} %get-tuple-element.59, bf16[512,288]{0,1:T(8,128)(2,1)S(1)} %get-tuple-element.58), kind=kOutput, calls=%fused_computation.13 | convolution fusion | flops 454557696 | bytes 2260992 | tf_op jit(solution)/shard_map/dot_general | solution.py:373
  76.2 1.6 convolution_convert_fusion.1
  77.8 1.7 %copy.38 = bf16[768,576]{1,0:T(8,128)(2,1)S(1)} copy(bf16[768,576]{0,1:T(8,128)(2,1)} %convolution_convert_fusion.1) | data formatting | bytes 1769472 | tf_op jit(solution)/shard_map/convert_element_type | solution.py:476
  79.5 1.3 copy.39
  80.8 1.9 %convolution_convert_fusion.5 = bf16[512,768]{1,0:T(8,128)(2,1)S(1)} fusion(bf16[512,288]{0,1:T(8,128)(2,1)} %copy-done.15, bf16[768,288]{1,0:T(8,128)(2,1)} %bitcast.116), kind=kOutput, calls=%fused_computation.15 | convolution fusion | flops 226885632 | bytes 1523712 | tf_op jit(solution)/shard_map/dot_general | solution.py:373
  82.7 29.5 %shard_map.154 = (f32[96,864]{1,0:T(8,128)S(1)}, bf16[128,768]{1,0:T(8,128)(2,1)S(1)}, f32[128,768]{1,0:T(8,128)S(1)}, bf16[4,128,768]{2,1,0:T(8,128)(2,1)S(1)}, f32[1,768]{1,0:T(1,128)S(1)}) custom-call(s32[1,2]{1,0:T(1,128)S(1)} %copy-done.11, bf16[8,96,576]{2,1,0:T(8,128)(2,1)S(1)} %bitcast.93, bf16[8,96,288]{2,1,0:T(8,128)(2,1)S(1)} %bitcast.98, ...), custom_call_target="tpu_custom_call" | custom-call | bytes 6985744 | tf_op jit(solution)/shard_map/pallas_call | solution.py:356
  113.3 1.0 slice_bitcast_fusion.2
  114.3 1.0 slice.99
  116.0 0.9 reshape.257
  117.0 2.6 %fusion.7 = bf16[512,1,3,64]{0,3,2,1:T(8,128)(2,1)S(1)} fusion(bf16[512,3,64]{0,2,1:T(8,128)(2,1)S(1)} %bitcast.125, f32[3,512,512]{1,2,0:T(8,128)} %get-tuple-element.83, f32[3,512]{1,0:T(4,128)S(1)} %copy-done.31), kind=kOutput, calls=%fused_computation.25 | convolution fusion | flops 102334464 | bytes 3545088 | tf_op jit(solution)/shard_map/hqk,qhd->khd/dot_general | solution.py:506
  119.8 1.6 %multiply_reduce_fusion = (f32[3,512]{1,0:T(4,128)S(1)}, f32[3,512,512]{1,2,0:T(8,128)S(1)}) fusion(f32[3,512,512]{1,2,0:T(8,128)S(1)} %copy-done.13, f32[3,512]{1,0:T(4,128)S(1)} %copy-done.31, bf16[512,3,64]{0,2,1:T(8,128)(2,1)S(1)} %bitcast.126, f32[512,3,3,64]{0,3,2,1:T(8,128)} %copy-done.12), kind=kOutput, calls=%fused_computation.2 | convolution fusion | flops 103021056 | bytes 6696960 | tf_op jit(solution)/shard_map/qhd,khd->hqk/dot_general | solution.py:509
  124.0 1.7 %convolution_convert_fusion.2 = bf16[512,768]{1,0:T(8,128)(2,1)} fusion(bf16[512,576]{0,1:T(8,128)(2,1)S(1)} %bitcast.120, bf16[768,576]{1,0:T(8,128)(2,1)S(1)} %bitcast.103), kind=kOutput, calls=%fused_computation.12 | convolution fusion | flops 453378048 | bytes 2260992 | tf_op jit(solution)/shard_map/dot_general | solution.py:373
  125.7 1.6 convolution_convert_fusion
  127.3 1.5 copy.43
  128.8 27.4 %shard_map.155 = (f32[96,768]{1,0:T(8,128)S(1)}, bf16[128,768]{1,0:T(8,128)(2,1)S(1)}, f32[8,768]{1,0:T(8,128)S(1)}) custom-call(bf16[8,96,576]{2,1,0:T(8,128)(2,1)S(1)} %bitcast.92, bf16[8,96,192]{2,1,0:T(8,128)(2,1)S(1)} %bitcast.99, bf16[4,128,768]{2,1,0:T(8,128)(2,1)S(1)} %bitcast.111, bf16[128,768]{1,0:T(8,128)(2,1)S(1)} %copy-done, ...), custom_call_target="tpu_custom_call" | custom-call | bytes 5124096 | tf_op jit(solution)/shard_map/pallas_call | solution.py:356
  157.9 0.9 copy.46
  (97 shorter events, 11.6 us)
Async XLA Ops:
  0.6 11.6 %copy-start.11 = (s32[1,2]{1,0:T(1,128)S(1)}, s32[1,2]{1,0:T(1,128)}, u32[]{:S(2)}) copy-start(s32[1,2]{1,0:T(1,128)} %lengths_ref.3) | copy-start | bytes 28
  0.6 11.6 %copy-start = (bf16[128,768]{1,0:T(8,128)(2,1)S(1)}, bf16[128,768]{1,0:T(8,128)(2,1)}, u32[]{:S(2)}) copy-start(bf16[128,768]{1,0:T(8,128)(2,1)} %x_ref.5) | copy-start | bytes 589828
  0.7 11.5 %copy-start.1 = (bf16[128,768]{1,0:T(8,128)(2,1)S(1)}, bf16[128,768]{1,0:T(8,128)(2,1)}, u32[]{:S(2)}) copy-start(bf16[128,768]{1,0:T(8,128)(2,1)} %cot_ref.3) | copy-start | bytes 589828
  35.2 3.2 %copy-start.2 = (bf16[4,128,768]{2,1,0:T(8,128)(2,1)}, bf16[4,128,768]{2,1,0:T(8,128)(2,1)S(1)}, u32[]{:S(2)}) copy-start(bf16[4,128,768]{2,1,0:T(8,128)(2,1)S(1)} %get-tuple-element.25) | copy-start | bytes 2359300
  36.5 2.9 %copy-start.18 = (f32[512,32]{0,1:T(8,128)S(1)}, f32[512,32]{0,1:T(8,128)}, u32[]{:S(2)}) copy-start(f32[512,32]{0,1:T(8,128)} %get-tuple-element.77) | copy-start | bytes 196612
  36.5 2.9 %copy-start.29 = (f32[512,32]{0,1:T(8,128)S(1)}, f32[512,32]{0,1:T(8,128)}, u32[]{:S(2)}) copy-start(f32[512,32]{0,1:T(8,128)} %get-tuple-element.76) | copy-start | bytes 196612
  38.4 1.0 copy-start.12
  39.6 4.0 %copy-start.20 = (bf16[512,3,32]{0,2,1:T(8,128)(2,1)}, bf16[512,3,32]{0,2,1:T(8,128)(2,1)S(1)}, u32[]{:S(2)}) copy-start(bf16[512,3,32]{0,2,1:T(8,128)(2,1)S(1)} %get-tuple-element.73) | copy-start | bytes 294916
  39.6 4.0 %copy-start.22 = (bf16[512,3,32]{0,2,1:T(8,128)(2,1)}, bf16[512,3,32]{0,2,1:T(8,128)(2,1)S(1)}, u32[]{:S(2)}) copy-start(bf16[512,3,32]{0,2,1:T(8,128)(2,1)S(1)} %get-tuple-element.74) | copy-start | bytes 294916
  39.6 4.0 %copy-start.24 = (bf16[512,3,32]{0,2,1:T(8,128)(2,1)}, bf16[512,3,32]{0,2,1:T(8,128)(2,1)S(1)}, u32[]{:S(2)}) copy-start(bf16[512,3,32]{0,2,1:T(8,128)(2,1)S(1)} %get-tuple-element.67) | copy-start | bytes 294916
  39.6 4.0 %copy-start.26 = (bf16[512,3,32]{0,2,1:T(8,128)(2,1)}, bf16[512,3,32]{0,2,1:T(8,128)(2,1)S(1)}, u32[]{:S(2)}) copy-start(bf16[512,3,32]{0,2,1:T(8,128)(2,1)S(1)} %get-tuple-element.68) | copy-start | bytes 294916
  43.6 2.4 %copy-start.30 = (f32[3,512]{1,0:T(4,128)}, f32[3,512]{1,0:T(4,128)S(1)}, u32[]{:S(2)}) copy-start(f32[3,512]{1,0:T(4,128)S(1)} %get-tuple-element.82) | copy-start | bytes 18436
  46.1 0.7 copy-start.16
  71.5 1.1 copy-start.9
  71.8 4.4 %copy-start.14 = (bf16[8,96,288]{2,1,0:T(8,128)(2,1)}, bf16[8,96,288]{2,1,0:T(8,128)(2,1)S(1)}, u32[]{:S(2)}) copy-start(bf16[8,96,288]{2,1,0:T(8,128)(2,1)S(1)} %slice.86) | copy-start | bytes 1327108
  73.2 3.0 %copy-start.15 = (bf16[512,288]{0,1:T(8,128)(2,1)}, bf16[512,288]{0,1:T(8,128)(2,1)S(1)}, u32[]{:S(2)}) copy-start(bf16[512,288]{0,1:T(8,128)(2,1)S(1)} %get-tuple-element.60) | copy-start | bytes 884740
  80.8 1.9 %copy-start.4 = (bf16[512,768]{1,0:T(8,128)(2,1)S(1)}, bf16[512,768]{1,0:T(8,128)(2,1)}, u32[]{:S(2)}) copy-start(bf16[512,768]{1,0:T(8,128)(2,1)} %convolution_convert_fusion.3) | copy-start | bytes 2359300
  80.8 1.9 %copy-start.10 = (f32[128,768]{1,0:T(8,128)S(1)}, f32[128,768]{1,0:T(8,128)}, u32[]{:S(2)}) copy-start(f32[128,768]{1,0:T(8,128)} %copy-done.9) | copy-start | bytes 1179652
  82.7 30.0 %copy-start.17 = (bf16[3,64,512]{2,1,0:T(8,128)(2,1)S(1)}, bf16[3,64,512]{2,1,0:T(8,128)(2,1)}, u32[]{:S(2)}) copy-start(bf16[3,64,512]{2,1,0:T(8,128)(2,1)} %copy-done.16) | copy-start | bytes 589828
  112.2 0.8 copy-start.6
  112.2 0.9 copy-start.7
  112.7 4.3 %copy-start.31 = (f32[3,512]{1,0:T(4,128)S(1)}, f32[3,512]{1,0:T(4,128)}, u32[]{:S(2)}) copy-start(f32[3,512]{1,0:T(4,128)} %copy-done.30) | copy-start | bytes 18436
  117.0 2.8 %copy-start.13 = (f32[3,512,512]{1,2,0:T(8,128)S(1)}, f32[3,512,512]{1,2,0:T(8,128)}, u32[]{:S(2)}) copy-start(f32[3,512,512]{1,2,0:T(8,128)} %get-tuple-element.83) | copy-start | bytes 9437188
  121.5 0.9 copy-start.25
  121.5 0.9 copy-start.27
  122.4 0.9 copy-start.21
  122.4 0.9 copy-start.23
  122.4 1.3 copy-start.19
  122.4 1.3 copy-start.28
  124.0 1.7 %copy-start.3 = (bf16[4,128,768]{2,1,0:T(8,128)(2,1)S(1)}, bf16[4,128,768]{2,1,0:T(8,128)(2,1)}, u32[]{:S(2)}) copy-start(bf16[4,128,768]{2,1,0:T(8,128)(2,1)} %copy-done.2) | copy-start | bytes 2359300
  125.7 3.1 %copy-start.5 = (bf16[512,768]{1,0:T(8,128)(2,1)S(1)}, bf16[512,768]{1,0:T(8,128)(2,1)}, u32[]{:S(2)}) copy-start(bf16[512,768]{1,0:T(8,128)(2,1)} %convolution_convert_fusion.2) | copy-start | bytes 2359300
  125.7 3.1 %copy-start.8 = (f32[128,768]{1,0:T(8,128)S(1)}, f32[128,768]{1,0:T(8,128)}, u32[]{:S(2)}) copy-start(f32[128,768]{1,0:T(8,128)} %copy-done.7) | copy-start | bytes 1179652

commit v4 on v3

--- a/solution.py
+++ b/solution.py
@@ -17,13 +17,12 @@
 
 
 def layout(lengths, row_count):
+    slots = jnp.arange(SEQS, dtype=jnp.int32)
+    ends = jnp.sum(jnp.where(slots[None, :] <= slots[:, None], lengths[None, :], 0), axis=1)
     row_ids = jnp.arange(row_count, dtype=jnp.int32)
-    segment, begin, end = jnp.zeros_like(row_ids), jnp.zeros_like(row_ids), 0
-    for slot in range(SEQS):
-        end = end + lengths[slot]
-        past = row_ids >= end
-        segment = segment + past.astype(jnp.int32)
-        begin = begin + jnp.where(past, lengths[slot], 0)
+    past = row_ids[None, :] >= ends[:, None]
+    segment = jnp.sum(past.astype(jnp.int32), axis=0)
+    begin = jnp.sum(jnp.where(past, lengths[:, None], 0), axis=0)
     return (segment, row_ids - begin)
 
 
@@ -139,28 +138,17 @@
 
 
 class Reduce:
-    def __init__(self, axis, count, me, parts, pair, sums, far, sems, pieces=()):
+    def __init__(self, axis, count, me, parts, pair, sums, far, sems):
         self.axis, self.count, self.me, self.parts = axis, count, me, parts
-        self.pieces = pieces
         self.pair, self.sums, self.far, self.sems = pair, sums, far, sems
         self.n_outer = count // 2
         self.first, self.second = {}, {}
         for step in list(range(1, self.n_outer)) + [0]:
             block = lax.rem(flip(me) + 2 * step, count)
-            self.pack(block)
             self.first[step] = send(
                 parts.at[block], pair.at[step], sems.at[0, step], sems.at[1, step],
                 {axis: flip(me)},
             )
-        for step in range(self.n_outer):
-            self.pack(lax.rem(me + 2 * step, count))
-
-    def pack(self, block):
-        column = 0
-        for piece in self.pieces:
-            width = piece.shape[2]
-            self.parts[block, :, column : column + width] = piece[block]
-            column += width
 
     def forward(self, step):
         self.first[step].wait_recv()
@@ -260,18 +248,16 @@
 
 
 def turn_kernel(
-    n_dp, n_t, lengths_ref, piece_one, piece_two, back_ref, out_part_ref, residual_ref, gain_ref,
+    n_dp, n_t, lengths_ref, grads, back_ref, out_part_ref, residual_ref, gain_ref,
     cot_ref,
     w_sum, output_ref, grad_residual_ref, grad_all, gain_part,
-    back_pair, back_sums, back_far, out_pair, out_sums, out_far, grads, pair, sums, far,
+    back_pair, back_sums, back_far, out_pair, out_sums, out_far, pair, sums, far,
     back_sems, out_sems, w_sems, row_sems,
 ):
     me, rank = lax.axis_index("dp"), lax.axis_index("tensor")
     greet(n_dp, n_t, me, rank)
     back = Reduce("tensor", n_t, rank, back_ref, back_pair, back_sums, back_far, back_sems)
-    weights = Reduce(
-        "dp", n_dp, me, grads, pair, sums, far, w_sems, (piece_one, piece_two)
-    )
+    weights = Reduce("dp", n_dp, me, grads, pair, sums, far, w_sems)
     forward_all([back])
     mlp_out = Reduce("tensor", n_t, rank, out_part_ref, out_pair, out_sums, out_far, out_sems)
     weights.forward(1)
@@ -300,17 +286,15 @@
 
 
 def last_kernel(
-    n_dp, n_t, piece_one, piece_two, back_ref, x_ref, gain_ref, grad_residual_ref, gain_part_ref,
+    n_dp, n_t, grads, back_ref, x_ref, gain_ref, grad_residual_ref, gain_part_ref,
     w_sum, input_grad_ref, gain_sum_ref,
-    back_pair, back_sums, back_far, grads, pair, sums, far, own_gain, near_gain, group_gain, far_gain,
+    back_pair, back_sums, back_far, pair, sums, far, own_gain, near_gain, group_gain, far_gain,
     back_sems, w_sems, near_sems, far_sems,
 ):
     me, rank = lax.axis_index("dp"), lax.axis_index("tensor")
     greet(n_dp, n_t, me, rank, all_dp=True)
     back = Reduce("tensor", n_t, rank, back_ref, back_pair, back_sums, back_far, back_sems)
-    weights = Reduce(
-        "dp", n_dp, me, grads, pair, sums, far, w_sems, (piece_one, piece_two)
-    )
+    weights = Reduce("dp", n_dp, me, grads, pair, sums, far, w_sems)
     forward_all([back])
     weights.forward(1)
     grad = back.total()
@@ -477,9 +461,7 @@
     wo2_grad = dot(grad_mlp_all, hidden, ((0,), (0,))).astype(low)
 
     def reduce_scratch(cols):
-        return [pltpu.VMEM((n_dp, depth, cols), low)] + [
-            pltpu.VMEM((n_outer, depth, cols), low)
-        ] * 3
+        return [pltpu.VMEM((n_outer, depth, cols), low)] * 3
 
     second_sum, output, grad_residual, grad_all, gain_part = call(
         turn_kernel, n_dp, n_t, 3,
@@ -494,8 +476,7 @@
         + [row_sems(), row_sems(), dma((4, n_outer)), row_sems()],
         (
             seq_lengths,
-            wi_grad.reshape(n_dp, depth, 2 * hidden_cols),
-            wo2_grad.reshape(n_dp, depth, wo2.shape[0]),
+            jnp.concatenate([wi_grad, wo2_grad], axis=1).reshape(n_dp, depth, second_cols),
             back_part.reshape(row_block), out_part.reshape(row_block),
             residual, gain_two, cotangent,
         ),
@@ -549,8 +530,7 @@
             row_sems(), dma((4, n_outer)), dma((2, n_t)), dma((2, n_dp)),
         ],
         (
-            wqkv_grad.reshape(n_dp, depth, 3 * head_cols),
-            wo_grad.reshape(n_dp, depth, wo.shape[0]),
+            jnp.concatenate([wqkv_grad, wo_grad], axis=1).reshape(n_dp, depth, first_cols),
             attn_back.reshape(row_block), inputs, gain_one, grad_residual, gain_part,
         ),
     )

time: 162 us -> 155 us (0.957)
  matrix products: 25.7 us -> 22 us
  local copies, waits for them, and re-layouts: 22 us -> 18.6 us
  other arithmetic: 5.28 us -> 7.79 us
    convert_element_type x4 -> x0, local copies, waits for them, and re-layouts: 4.73 us -> none  [the longest x1 1.71 us: shards(): wi_grad = dot(mlp_all, grad_proj, ((0,), (0,))).astype(low)]
    dot_general x12, matrix products: 14 us -> 10.3 us  [dot(): lax.dot_general(first, second, (dims, ((), ())), preferred_element_type=j...]
    concatenate x0 -> x2, local copies, waits for them, and re-layouts: none -> 3.58 us  [the longest x1 1.96 us: shards(): jnp.concatenate([wi_grad, wo2_grad], axis=1)]
    concatenate x0 -> x2, other arithmetic: none -> 2.29 us  [the longest x1 1.16 us: shards(): jnp.concatenate([wi_grad, wo2_grad], axis=1)]
    unnamed x72 -> x68, local copies, waits for them, and re-layouts: 8.7 us -> 9.61 us
where the time goes in v4:
time: 155 us; the launch traced here: 154 us
  Pallas kernels  104 us (67%)
  matrix products  22 us (14%)
  local copies, waits for them, and re-layouts  18.6 us (12%)
  other arithmetic  7.79 us (5%)
    pallas_call x4, Pallas kernels, call(): pl.pallas_call(functools.partial(kernel, n_dp, n_t), out_shape=[jax.Shape...  104 us
    dot_general x12, matrix products, dot(): lax.dot_general(first, second, (dims, ((), ())), preferred_element_type=j...  10.3 us
    unnamed x68, local copies, waits for them, and re-layouts  9.61 us
    sub x1, matrix products, shards(): exponent = jnp.exp(scores - jnp.max(scores, axis=-1, keepdims=True))  3.98 us

profile of v4, /device:TPU:11, one launch (start us, length us, event | category | flops | bytes accessed | tf_op | source)
XLA Modules:
  0.0 154.1 jit_solution(12464220986136805404)
XLA Ops:
  0.7 0.7 pad_maximum_fusion.21
  1.4 0.8 fusion.24
  2.2 0.7 select_reduce_fusion
  3.5 0.9 copy.47
  4.4 1.0 copy.45
  5.4 1.1 reshape.208
  6.6 1.1 copy.46
  7.9 1.0 fusion.23
  8.9 0.9 broadcast_compare_fusion
  9.8 23.0 %shard_map.152 = (bf16[8,96,576]{2,1,0:T(8,128)(2,1)S(1)}, bf16[8,96,192]{2,1,0:T(8,128)(2,1)S(1)}, bf16[4,128,768]{2,1,0:T(8,128)(2,1)S(1)}, bf16[4,128,768]{2,...) custom-call(s32[1,2]{1,0:T(1,128)S(1)} %copy-done.9, bf16[112,768]{1,0:T(8,128)(2,1)S(1)} %maximum_maximum_fusion.w_ref, ...), custom_call_target="tpu_custom_call" | custom-call | bytes 1130512 | tf_op jit(solution)/shard_map/pallas_call | solution.py:340
  32.8 1.3 copy.49
  34.2 1.9 %fusion.36 = f32[512,3,3,64]{0,3,2,1:T(8,128)S(1)} fusion(bf16[512,768,1,1]{1,0,3,2:T(8,128)(2,1)S(1)} %bitcast.101, bf16[3,3,64,768]{3,2,1,0:T(8,128)(2,1)} %bitcast.111), kind=kOutput, calls=%fused_computation.90 | convolution fusion | flops 452984832 | bytes 2850816 | tf_op jit(solution)/shard_map/dot_general | solution.py:357
  36.1 1.0 copy-done.10
  37.3 4.0 %fusion.35 = (f32[3,512]{1,0:T(4,128)S(1)}, f32[3,512,512]{1,2,0:T(8,128)}) fusion(pred[512,512]{0,1:T(8,128)(4,1)} %broadcast_compare_fusion, bf16[512,3,32]{0,2,1:T(8,128)(2,1)S(1)} %get-tuple-element.83, bf16[512,3,32]{0,2,1:T(8,128)(2,1)S(1)} %get-tuple-element.84, bf16[512,3,32]{0,2,1:T(8,128)(2,1)S(1)} %get-tuple-element.78, ...), kind=kOutput, calls=%fused_computation.89 | convolution fusion | flops 104595968 | bytes 3807232 | tf_op jit(solution)/shard_map/sub | solution.py:424
  41.3 2.4 %convolution_convert_fusion.10 = bf16[3,64,512]{2,1,0:T(8,128)(2,1)S(1)} fusion(f32[512,3,3,64]{0,3,2,1:T(8,128)} %copy-done.10, f32[3,512,512]{1,2,0:T(8,128)} %get-tuple-element.91, f32[3,512]{1,0:T(4,128)S(1)} %get-tuple-element.90), kind=kOutput, calls=%fused_computation.26 | convolution fusion | flops 102334464 | bytes 3545088 | tf_op jit(solution)/shard_map/hqk,khd->qhd/dot_general | solution.py:428
  44.2 24.7 %shard_map.153 = (bf16[8,96,864]{2,1,0:T(8,128)(2,1)S(1)}, f32[128,768]{1,0:T(8,128)S(1)}, bf16[4,128,768]{2,1,0:T(8,128)(2,1)S(1)}) custom-call(bf16[96,864]{1,0:T(8,128)(2,1)S(1)} %pad_maximum_fusion.8.w_ref, bf16[4,128,768]{2,1,0:T(8,128)(2,1)S(1)} %bitcast.93, bf16[128,768]{1,0:T(8,128)(2,1)S(1)} %copy-done, f32[1,768]{1,0:T(1,128)S(1)} %get-tuple-element.28.gain_ref), custom_call_target="tpu_custom_call" | custom-call | bytes 2304000 | tf_op jit(solution)/shard_map/pallas_call | solution.py:340
  71.4 1.7 %convolution_convert_fusion.3 = bf16[512,768]{1,0:T(8,128)(2,1)} fusion(bf16[768,576]{1,0:T(8,128)(2,1)S(1)} %bitcast.110, bf16[512,288]{0,1:T(8,128)(2,1)S(1)} %get-tuple-element.69, bf16[512,288]{0,1:T(8,128)(2,1)S(1)} %get-tuple-element.68), kind=kOutput, calls=%fused_computation.13 | convolution fusion | flops 454557696 | bytes 2260992 | tf_op jit(solution)/shard_map/dot_general | solution.py:357
  73.8 1.2 pad_maximum_fusion
  74.9 2.0 %copy.51 = bf16[768,864]{1,0:T(8,128)(2,1)S(1)} copy(bf16[768,864]{0,1:T(8,128)(2,1)} %pad_maximum_fusion) | data formatting | bytes 2654208 | tf_op jit(solution)/shard_map/concatenate | solution.py:479
  76.9 1.9 %convolution_convert_fusion.5 = bf16[512,768]{1,0:T(8,128)(2,1)S(1)} fusion(bf16[512,288]{0,1:T(8,128)(2,1)} %copy-done.13, bf16[768,288]{1,0:T(8,128)(2,1)} %bitcast.113), kind=kOutput, calls=%fused_computation.15 | convolution fusion | flops 226885632 | bytes 1523712 | tf_op jit(solution)/shard_map/dot_general | solution.py:357
  78.8 29.4 %shard_map.154 = (f32[96,864]{1,0:T(8,128)S(1)}, bf16[128,768]{1,0:T(8,128)(2,1)S(1)}, f32[128,768]{1,0:T(8,128)S(1)}, bf16[4,128,768]{2,1,0:T(8,128)(2,1)S(1)}, f32[1,768]{1,0:T(1,128)S(1)}) custom-call(s32[1,2]{1,0:T(1,128)S(1)} %copy-done.9, bf16[8,96,864]{2,1,0:T(8,128)(2,1)S(1)} %bitcast.89, bf16[4,128,768]{2,1,0:T(8,128)(2,1)S(1)} %bitcast.106, ...), custom_call_target="tpu_custom_call" | custom-call | bytes 6985744 | tf_op jit(solution)/shard_map/pallas_call | solution.py:340
  109.1 0.8 copy.59
  109.9 0.9 reshape.227
  110.9 2.6 %fusion.7 = bf16[512,1,3,64]{0,3,2,1:T(8,128)(2,1)S(1)} fusion(bf16[512,3,64]{0,2,1:T(8,128)(2,1)S(1)} %bitcast.122, f32[3,512,512]{1,2,0:T(8,128)} %get-tuple-element.91, f32[3,512]{1,0:T(4,128)S(1)} %copy-done.29), kind=kOutput, calls=%fused_computation.27 | convolution fusion | flops 102334464 | bytes 3545088 | tf_op jit(solution)/shard_map/hqk,qhd->khd/dot_general | solution.py:487
  113.7 1.6 %multiply_reduce_fusion = (f32[3,512]{1,0:T(4,128)S(1)}, f32[3,512,512]{1,2,0:T(8,128)S(1)}) fusion(f32[3,512,512]{1,2,0:T(8,128)S(1)} %copy-done.11, f32[3,512]{1,0:T(4,128)S(1)} %copy-done.29, bf16[512,3,64]{0,2,1:T(8,128)(2,1)S(1)} %bitcast.123, f32[512,3,3,64]{0,3,2,1:T(8,128)} %copy-done.10), kind=kOutput, calls=%fused_computation.2 | convolution fusion | flops 103021056 | bytes 6696960 | tf_op jit(solution)/shard_map/qhd,khd->hqk/dot_general | solution.py:490
  115.4 0.8 multiply_convert_fusion
  118.3 0.8 convolution_convert_fusion.2
  120.1 1.1 pad_maximum_fusion.1
  121.2 1.6 %copy.55 = bf16[768,768]{1,0:T(8,128)(2,1)S(1)} copy(bf16[768,768]{0,1:T(8,128)(2,1)} %pad_maximum_fusion.1) | data formatting | bytes 2359296 | tf_op jit(solution)/shard_map/concatenate | solution.py:533
  122.9 27.3 %shard_map.155 = (f32[96,768]{1,0:T(8,128)S(1)}, bf16[128,768]{1,0:T(8,128)(2,1)S(1)}, f32[8,768]{1,0:T(8,128)S(1)}) custom-call(bf16[8,96,768]{2,1,0:T(8,128)(2,1)S(1)} %bitcast.90, bf16[4,128,768]{2,1,0:T(8,128)(2,1)S(1)} %bitcast.105, bf16[128,768]{1,0:T(8,128)(2,1)S(1)} %copy-done, f32[1,768]{1,0:T(1,128)S(1)} %get-tuple-element.35.gain_ref, ...), custom_call_target="tpu_custom_call" | custom-call | bytes 5124096 | tf_op jit(solution)/shard_map/pallas_call | solution.py:340
  150.9 0.7 copy.58
  151.8 0.9 copy.57
  (93 shorter events, 11.0 us)
Async XLA Ops:
  0.6 9.2 %copy-start.9 = (s32[1,2]{1,0:T(1,128)S(1)}, s32[1,2]{1,0:T(1,128)}, u32[]{:S(2)}) copy-start(s32[1,2]{1,0:T(1,128)} %lengths_ref.3) | copy-start | bytes 28
  0.6 9.2 %copy-start = (bf16[128,768]{1,0:T(8,128)(2,1)S(1)}, bf16[128,768]{1,0:T(8,128)(2,1)}, u32[]{:S(2)}) copy-start(bf16[128,768]{1,0:T(8,128)(2,1)} %x_ref.5) | copy-start | bytes 589828
  0.7 9.1 %copy-start.4 = (bf16[128,768]{1,0:T(8,128)(2,1)S(1)}, bf16[128,768]{1,0:T(8,128)(2,1)}, u32[]{:S(2)}) copy-start(bf16[128,768]{1,0:T(8,128)(2,1)} %cot_ref.3) | copy-start | bytes 589828
  32.8 3.2 %copy-start.1 = (bf16[4,128,768]{2,1,0:T(8,128)(2,1)}, bf16[4,128,768]{2,1,0:T(8,128)(2,1)S(1)}, u32[]{:S(2)}) copy-start(bf16[4,128,768]{2,1,0:T(8,128)(2,1)S(1)} %get-tuple-element.25) | copy-start | bytes 2359300
  34.2 2.9 %copy-start.16 = (f32[512,32]{0,1:T(8,128)S(1)}, f32[512,32]{0,1:T(8,128)}, u32[]{:S(2)}) copy-start(f32[512,32]{0,1:T(8,128)} %get-tuple-element.87) | copy-start | bytes 196612
  34.2 2.9 %copy-start.27 = (f32[512,32]{0,1:T(8,128)S(1)}, f32[512,32]{0,1:T(8,128)}, u32[]{:S(2)}) copy-start(f32[512,32]{0,1:T(8,128)} %get-tuple-element.86) | copy-start | bytes 196612
  36.0 1.1 copy-start.10
  37.2 4.0 %copy-start.18 = (bf16[512,3,32]{0,2,1:T(8,128)(2,1)}, bf16[512,3,32]{0,2,1:T(8,128)(2,1)S(1)}, u32[]{:S(2)}) copy-start(bf16[512,3,32]{0,2,1:T(8,128)(2,1)S(1)} %get-tuple-element.83) | copy-start | bytes 294916
  37.2 4.0 %copy-start.20 = (bf16[512,3,32]{0,2,1:T(8,128)(2,1)}, bf16[512,3,32]{0,2,1:T(8,128)(2,1)S(1)}, u32[]{:S(2)}) copy-start(bf16[512,3,32]{0,2,1:T(8,128)(2,1)S(1)} %get-tuple-element.84) | copy-start | bytes 294916
  37.3 4.0 %copy-start.22 = (bf16[512,3,32]{0,2,1:T(8,128)(2,1)}, bf16[512,3,32]{0,2,1:T(8,128)(2,1)S(1)}, u32[]{:S(2)}) copy-start(bf16[512,3,32]{0,2,1:T(8,128)(2,1)S(1)} %get-tuple-element.77) | copy-start | bytes 294916
  37.3 4.0 %copy-start.24 = (bf16[512,3,32]{0,2,1:T(8,128)(2,1)}, bf16[512,3,32]{0,2,1:T(8,128)(2,1)S(1)}, u32[]{:S(2)}) copy-start(bf16[512,3,32]{0,2,1:T(8,128)(2,1)S(1)} %get-tuple-element.78) | copy-start | bytes 294916
  41.3 2.4 %copy-start.28 = (f32[3,512]{1,0:T(4,128)}, f32[3,512]{1,0:T(4,128)S(1)}, u32[]{:S(2)}) copy-start(f32[3,512]{1,0:T(4,128)S(1)} %get-tuple-element.90) | copy-start | bytes 18436
  43.7 25.5 %copy-start.14 = (bf16[3,64,512]{2,1,0:T(8,128)(2,1)}, bf16[3,64,512]{2,1,0:T(8,128)(2,1)S(1)}, u32[]{:S(2)}) copy-start(bf16[3,64,512]{2,1,0:T(8,128)(2,1)S(1)} %convolution_convert_fusion.10) | copy-start | bytes 589828
  68.9 0.8 copy-start.7
  69.2 1.2 copy-start.12
  71.0 2.1 %copy-start.13 = (bf16[512,288]{0,1:T(8,128)(2,1)}, bf16[512,288]{0,1:T(8,128)(2,1)S(1)}, u32[]{:S(2)}) copy-start(bf16[512,288]{0,1:T(8,128)(2,1)S(1)} %get-tuple-element.70) | copy-start | bytes 884740
  76.9 1.9 %copy-start.3 = (bf16[512,768]{1,0:T(8,128)(2,1)S(1)}, bf16[512,768]{1,0:T(8,128)(2,1)}, u32[]{:S(2)}) copy-start(bf16[512,768]{1,0:T(8,128)(2,1)} %convolution_convert_fusion.3) | copy-start | bytes 2359300
  76.9 1.9 %copy-start.8 = (f32[128,768]{1,0:T(8,128)S(1)}, f32[128,768]{1,0:T(8,128)}, u32[]{:S(2)}) copy-start(f32[128,768]{1,0:T(8,128)} %copy-done.7) | copy-start | bytes 1179652
  78.8 29.8 %copy-start.15 = (bf16[3,64,512]{2,1,0:T(8,128)(2,1)S(1)}, bf16[3,64,512]{2,1,0:T(8,128)(2,1)}, u32[]{:S(2)}) copy-start(bf16[3,64,512]{2,1,0:T(8,128)(2,1)} %copy-done.14) | copy-start | bytes 589828
  108.2 0.8 copy-start.5
  108.7 2.2 %copy-start.29 = (f32[3,512]{1,0:T(4,128)S(1)}, f32[3,512]{1,0:T(4,128)}, u32[]{:S(2)}) copy-start(f32[3,512]{1,0:T(4,128)} %copy-done.28) | copy-start | bytes 18436
  110.9 2.8 %copy-start.11 = (f32[3,512,512]{1,2,0:T(8,128)S(1)}, f32[3,512,512]{1,2,0:T(8,128)}, u32[]{:S(2)}) copy-start(f32[3,512,512]{1,2,0:T(8,128)} %get-tuple-element.91) | copy-start | bytes 9437188
  115.3 0.9 copy-start.23
  115.3 0.9 copy-start.25
  116.3 0.9 copy-start.19
  116.3 0.9 copy-start.21
  117.2 0.8 copy-start.17
  117.2 0.9 copy-start.26
  118.3 1.1 copy-start.2
  121.2 1.6 %copy-start.6 = (f32[128,768]{1,0:T(8,128)S(1)}, f32[128,768]{1,0:T(8,128)}, u32[]{:S(2)}) copy-start(f32[128,768]{1,0:T(8,128)} %copy-done.5) | copy-start | bytes 1179652
